TPU v7x, 256 devices: a whole 4x4x8 slice. The times are simulated.
256 devices in a mesh: ctx: 32 (over x, z), tp: 8 (over y, core).
Axes of the slice: x: 4, y: 4, z: 8, core: 2. Of those that a mesh axis runs over, the one named last changes fastest.
Arguments:
- doc_lengths: int32 [32], replicated, may hold values from 1 to 1024, 16384 in all
- activations: bfloat16 [16384, 4096], P('ctx'), may hold values from -0.09375 to 0.09375
- queries: bfloat16 [16384, 4096], P('ctx', 'tp'), may hold values from -4.6 to 4.6
- key_heads: bfloat16 [16384, 1024], P('ctx', 'tp'), may hold values from -4.6 to 4.6
- head_values: bfloat16 [16384, 1024], P('ctx', 'tp'), may hold values from -6 to 6
- output_gradient: bfloat16 [16384, 4096], P('ctx', 'tp'), may hold values from -6 to 6
Outputs:
- query_weight_grad: bfloat16 [4096, 4096], P('ctx', 'tp')
- key_weight_grad: bfloat16 [4096, 1024], P('ctx', 'tp')
- value_weight_grad: bfloat16 [4096, 1024], P('ctx', 'tp')
Inputs may be any that keep to these rules, and one draw needn't show every extreme that they name: `doc_lengths`: the lengths sum to 16384; the longest document has exactly 1024 tokens.
All inputs are finite; a program needn't handle non-finite values.
Results may differ from a plain program's by a relative error of at most 0.025.
Values may be sent and summed in bfloat16 or wider, within the bound.
A program may use at most 64 MiB of HBM per device.

v0:
```python
import jax
import jax.numpy as jnp
from jax import lax
from jax.sharding import PartitionSpec as P

HEAD_SIZE = 128
SPAN = 2


def passed_along(value, axis, steps):
    count = lax.axis_size(axis)
    initial, last = (max(0, -steps), min(count, count - steps))
    return lax.ppermute(value, axis, [(source, source + steps) for source in range(initial, last)])


def doc_index(doc_ends, positions):
    return jnp.sum((doc_ends[None, :] <= positions[:, None]).astype(jnp.int32), axis=1)


def weight_term(activations, grads):
    return lax.dot_general(
        activations, grads, (((0,), (0,)), ((), ())), preferred_element_type=jnp.float32
    )


def shards(doc_lengths, activations, queries, key_heads, head_values, output_gradient):
    tok_rows = key_heads.shape[0]
    key_value_width = key_heads.shape[1]
    query_group_size = queries.shape[1] // key_value_width
    group_width = query_group_size * HEAD_SIZE
    att_scale = HEAD_SIZE ** (-0.5)
    first_pos = lax.axis_index("ctx") * tok_rows
    doc_ends = jnp.cumsum(doc_lengths)
    query_pos = first_pos + jnp.arange(tok_rows, dtype=jnp.int32)
    key_pos = first_pos - SPAN * tok_rows + jnp.arange((SPAN + 1) * tok_rows, dtype=jnp.int32)
    same_doc = doc_index(doc_ends, query_pos)[:, None] == doc_index(doc_ends, key_pos)[None, :]
    visible = same_doc & (key_pos[None, :] <= query_pos[:, None]) & (key_pos[None, :] >= 0)
    packed = jnp.concatenate([key_heads, head_values], axis=1)
    remote = [passed_along(packed, "ctx", distance) for distance in range(1, SPAN + 1)]
    span_rows = jnp.concatenate(remote[::-1] + [packed], axis=0)
    key_span_rows = span_rows[:, :key_value_width]
    value_span_rows = span_rows[:, key_value_width:]
    query_group = queries.reshape(tok_rows, query_group_size, HEAD_SIZE)
    grad_group = output_gradient.reshape(tok_rows, query_group_size, HEAD_SIZE)
    scores = (
        jnp.einsum("tgd,kd->gtk", query_group, key_span_rows, preferred_element_type=jnp.float32)
        * att_scale
    )
    scores = jnp.where(visible[None], scores, -jnp.inf)
    row_max = jnp.max(scores, axis=-1, keepdims=True)
    weights = jnp.exp(scores - row_max)
    probs = weights / jnp.sum(weights, axis=-1, keepdims=True)
    probs_low = probs.astype(jnp.bfloat16)
    attended = jnp.einsum(
        "gtk,kd->gtd", probs_low, value_span_rows, preferred_element_type=jnp.float32
    )
    delta = jnp.sum(jnp.transpose(grad_group, (1, 0, 2)).astype(jnp.float32) * attended, axis=-1)
    dprobs = jnp.einsum(
        "tgd,kd->gtk", grad_group, value_span_rows, preferred_element_type=jnp.float32
    )
    dscores = probs * (dprobs - delta[..., None])
    dscores_low = dscores.astype(jnp.bfloat16)
    query_grad = (
        jnp.einsum("gtk,kd->tgd", dscores_low, key_span_rows, preferred_element_type=jnp.float32)
        * att_scale
    )
    key_grad = (
        jnp.einsum("gtk,tgd->kd", dscores_low, query_group, preferred_element_type=jnp.float32)
        * att_scale
    )
    value_grad = jnp.einsum(
        "gtk,tgd->kd", probs_low, grad_group, preferred_element_type=jnp.float32
    )
    query_parts = query_grad.reshape(tok_rows, group_width)
    query_low = query_parts.astype(jnp.bfloat16)
    kv_grad = jnp.concatenate([key_grad, value_grad], axis=1)
    far_terms = [
        kv_grad[(SPAN - 1 - offset) * tok_rows : (SPAN - offset) * tok_rows]
        for offset in range(SPAN)
    ]
    local_part = kv_grad[SPAN * tok_rows :]
    returned = local_part
    for distance in range(1, SPAN + 1):
        returned = returned + passed_along(
            far_terms[distance - 1].astype(jnp.bfloat16), "ctx", -distance
        ).astype(jnp.float32)
    kv_low = returned.astype(jnp.bfloat16)
    joined = jnp.concatenate([query_low, kv_low], axis=1)
    all_grads = lax.psum_scatter(
        weight_term(activations, joined).astype(jnp.bfloat16),
        "ctx",
        scatter_dimension=0,
        tiled=True,
    )
    query_weight_grad = all_grads[:, : query_low.shape[1]]
    kv_weight_grad = all_grads[:, query_low.shape[1] :]
    return (
        query_weight_grad,
        kv_weight_grad[:, :key_value_width],
        kv_weight_grad[:, key_value_width:],
    )


def solution(mesh):
    return jax.shard_map(
        shards,
        mesh=mesh,
        in_specs=(
            P(),
            P("ctx", None),
            P("ctx", "tp"),
            P("ctx", "tp"),
            P("ctx", "tp"),
            P("ctx", "tp"),
        ),
        out_specs=(P("ctx", "tp"), P("ctx", "tp"), P("ctx", "tp")),
        check_vma=False,
    )
```

profile of v0, /device:TPU:32, one launch (start us, length us, event | category | flops | bytes accessed | tf_op | source)
XLA Modules:
  0.0 337.2 jit_solution(13456229328026130183)
XLA Ops:
  7.2 0.9 constant_dynamic-update-slice_fusion.1
  8.1 0.9 constant_dynamic-update-slice_fusion
  9.1 5.2 %collective-permute-start = (bf16[512,256]{1,0:T(8,128)(2,1)S(1)}, bf16[512,256]{1,0:T(8,128)(2,1)S(1)}, u32[]{:S(2)}, u32[]{:S(2)}) collective-permute-start(bf16[512,256]{1,0:T(8,128)(2,1)S(1)} %constant_dynamic-update-slice_fusion), channel_id=1, source_target_pairs={{0,16},{8,24},{16,32},{24,40},{32,48},{40,56},{48,64},{56,72},{64,... | collective-permute-start | bytes 786440 | tf_op jit(solution)/shard_map/ppermute | solution.py:13
  14.3 5.0 %collective-permute-start.1 = (bf16[512,256]{1,0:T(8,128)(2,1)S(1)}, bf16[512,256]{1,0:T(8,128)(2,1)S(1)}, u32[]{:S(2)}, u32[]{:S(2)}) collective-permute-start(bf16[512,256]{1,0:T(8,128)(2,1)S(1)} %constant_dynamic-update-slice_fusion), channel_id=1, source_target_pairs={{0,8},{8,16},{16,24},{24,32},{32,40},{40,48},{48,56},{56,64},{64,7... | collective-permute-start | bytes 786440 | tf_op jit(solution)/shard_map/ppermute | solution.py:13
  19.4 0.7 copy.51
  20.1 0.1 reduce-window.8
  20.2 0.1 reduce
  20.3 0.1 convert_reduce_fusion
  20.4 0.1 convert_reduce_fusion.1
  20.5 1.3 copy.79
  21.7 1.3 copy.53
  23.0 2.3 and_and_fusion
  25.3 6.4 %collective-permute-done.1 = bf16[512,256]{1,0:T(8,128)(2,1)S(1)} collective-permute-done((bf16[512,256]{1,0:T(8,128)(2,1)S(1)}, bf16[512,256]{1,0:T(8,128)(2,1)S(1)}, u32[]{:S(2)}, u32[]{:S(2)}) %collective-permute-start.1) | collective-permute-done | bytes 262176 | tf_op jit(solution)/shard_map/ppermute | solution.py:13
  31.7 1.8 fusion.20
  33.5 10.0 %fusion.26 = (f32[4,512]{1,0:T(4,128)S(1)}, f32[4,512,1536]{1,2,0:T(8,128)}) fusion(f32[1536,512,4]{1,0,2:T(8,128)S(1)} %fusion.20, pred[512,1536]{0,1:T(8,128)(4,1)} %and_and_fusion), kind=kOutput, calls=%fused_computation.49 | output fusion | flops 18875904 | bytes 25960448 | tf_op jit(solution)/shard_map/sub | solution.py:51
  43.5 9.0 %fusion.8 = bf16[4,512,1536]{1,2,0:T(8,128)(2,1)} fusion(f32[4,512,1536]{1,2,0:T(8,128)} %get-tuple-element.20, f32[4,512]{1,0:T(4,128)S(1)} %get-tuple-element.19), kind=kLoop, calls=%fused_computation.13 | loop fusion | flops 6291456 | bytes 18882560 | tf_op jit(solution)/shard_map/convert_element_type | solution.py:53
  52.5 4.0 %fusion.12 = f32[4,512]{1,0:T(4,128)S(1)} fusion(bf16[4,512,1536]{1,2,0:T(8,128)(2,1)} %fusion.8, bf16[512,4,128]{0,2,1:T(8,128)(2,1)S(1)} %bitcast.56, bf16[1536,256]{1,0:T(8,128)(2,1)S(1)} %pad_maximum_fusion.1), kind=kOutput, calls=%fused_computation.25 | convolution fusion | flops 806090752 | bytes 7217152 | tf_op jit(solution)/shard_map/gtk,kd->gtd/dot_general | solution.py:54
  56.5 5.6 %convolution_bitcast_fusion = f32[1536,128]{0,1:T(8,128)S(1)} fusion(bf16[4,512,1536]{1,2,0:T(8,128)(2,1)} %fusion.8, bf16[512,4,128]{0,2,1:T(8,128)(2,1)S(1)} %bitcast.57), kind=kOutput, calls=%fused_computation.15 | convolution fusion | flops 805306368 | bytes 7602176 | tf_op jit(solution)/shard_map/gtk,tgd->kd/dot_general | solution.py:71
  62.1 2.0 fusion.2
  64.1 2.1 fusion.9
  66.2 0.1 fusion.10
  66.4 2.2 collective-permute-start.2
  68.6 1.5 collective-permute-start.3
  70.1 1.0 fusion.11
  71.1 7.5 %collective-permute-done.2 = bf16[512,256]{0,1:T(8,128)(2,1)S(1)} collective-permute-done((bf16[512,256]{0,1:T(8,128)(2,1)S(1)}, bf16[512,256]{0,1:T(8,128)(2,1)S(1)}, u32[]{:S(2)}, u32[]{:S(2)}) %collective-permute-start.2) | collective-permute-done | bytes 262176 | tf_op jit(solution)/shard_map/ppermute | solution.py:13
  78.6 7.5 %collective-permute-done.3 = bf16[512,256]{0,1:T(8,128)(2,1)S(1)} collective-permute-done((bf16[512,256]{0,1:T(8,128)(2,1)S(1)}, bf16[512,256]{0,1:T(8,128)(2,1)S(1)}, u32[]{:S(2)}, u32[]{:S(2)}) %collective-permute-start.3) | collective-permute-done | bytes 262176 | tf_op jit(solution)/shard_map/ppermute | solution.py:13
  86.1 0.1 fusion.19
  86.2 5.4 %fusion.7 = bf16[4096,768]{0,1:T(8,128)(2,1)} fusion(bf16[512,4096]{1,0:T(8,128)(2,1)S(1)} %copy-done.1, bf16[512,256]{0,1:T(8,128)(2,1)S(1)} %fusion.19, bf16[512,512]{0,1:T(8,128)(2,1)S(1)} %bitcast.55), kind=kOutput, calls=%fused_computation.12 | convolution fusion | flops 3225944064 | bytes 11272192 | tf_op jit(solution)/shard_map/dot_general | solution.py:21
  91.6 8.7 %copy.74 = bf16[4096,768]{1,0:T(8,128)(2,1)} copy(bf16[4096,768]{0,1:T(8,128)(2,1)} %fusion.7) | data formatting | bytes 12582912
  100.3 227.1 %reduce-scatter.4.cloned.1.call-done = bf16[128,768]{1,0:T(8,128)(2,1)} async-done(((bf16[4096,768]{1,0:T(8,128)(2,1)}), bf16[128,768]{1,0:T(8,128)(2,1)}) %reduce-scatter.4.cloned.1.call-update) | async-done | bytes 196624
  327.4 1.6 slice.43
  328.9 1.4 fusion.25
  (12 shorter events, 0.2 us)
Async XLA Ops:
  7.2 320.2 %reduce-scatter.4.cloned.1.call-start = ((), (), s32[]{:S(2)}) async-start(), calls=%async_computation.1 | async-start | bytes 6488064
  9.1 16.2 %collective-permute-start = (bf16[512,256]{1,0:T(8,128)(2,1)S(1)}, bf16[512,256]{1,0:T(8,128)(2,1)S(1)}, u32[]{:S(2)}, u32[]{:S(2)}) collective-permute-start(bf16[512,256]{1,0:T(8,128)(2,1)S(1)} %constant_dynamic-update-slice_fusion), channel_id=1, source_target_pairs={{0,16},{8,24},{16,32},{24,40},{32,48},{40,56},{48,64},{56,72},{64,... | collective-permute-start | bytes 786440 | tf_op jit(solution)/shard_map/ppermute | solution.py:13
  14.3 17.4 %collective-permute-start.1 = (bf16[512,256]{1,0:T(8,128)(2,1)S(1)}, bf16[512,256]{1,0:T(8,128)(2,1)S(1)}, u32[]{:S(2)}, u32[]{:S(2)}) collective-permute-start(bf16[512,256]{1,0:T(8,128)(2,1)S(1)} %constant_dynamic-update-slice_fusion), channel_id=1, source_target_pairs={{0,8},{8,16},{16,24},{24,32},{32,40},{40,48},{48,56},{56,64},{64,7... | collective-permute-start | bytes 786440 | tf_op jit(solution)/shard_map/ppermute | solution.py:13
  52.5 9.6 %copy-start = (f32[4,512,1536]{1,2,0:T(8,128)S(1)}, f32[4,512,1536]{1,2,0:T(8,128)}, u32[]{:S(2)}) copy-start(f32[4,512,1536]{1,2,0:T(8,128)} %get-tuple-element.20) | copy-start | bytes 37748740
  66.2 20.0 %copy-start.1 = (bf16[512,4096]{1,0:T(8,128)(2,1)S(1)}, bf16[512,4096]{1,0:T(8,128)(2,1)}, u32[]{:S(2)}) copy-start(bf16[512,4096]{1,0:T(8,128)(2,1)} %param.7) | copy-start | bytes 12582916
  66.4 12.2 %collective-permute-start.2 = (bf16[512,256]{0,1:T(8,128)(2,1)S(1)}, bf16[512,256]{0,1:T(8,128)(2,1)S(1)}, u32[]{:S(2)}, u32[]{:S(2)}) collective-permute-start(bf16[512,256]{0,1:T(8,128)(2,1)S(1)} %get-tuple-element.15), channel_id=1, source_target_pairs={{8,0},{16,8},{24,16},{32,24},{40,32},{48,40},{56,48},{64,56},{72,6... | collective-permute-start | bytes 786440 | tf_op jit(solution)/shard_map/ppermute | solution.py:13
  68.6 17.5 %collective-permute-start.3 = (bf16[512,256]{0,1:T(8,128)(2,1)S(1)}, bf16[512,256]{0,1:T(8,128)(2,1)S(1)}, u32[]{:S(2)}, u32[]{:S(2)}) collective-permute-start(bf16[512,256]{0,1:T(8,128)(2,1)S(1)} %get-tuple-element.16), channel_id=1, source_target_pairs={{16,0},{24,8},{32,16},{40,24},{48,32},{56,40},{64,48},{72,56},{80,... | collective-permute-start | bytes 786440 | tf_op jit(solution)/shard_map/ppermute | solution.py:13
Sparse Core Ops, SparseCore 0:
  100.4 226.9 reduce-scatter.3
where the time goes:
time: 339 us; the launch traced here: 337 us
  waiting for transfers between devices  248 us (73%)
  other arithmetic  22 us (6%)
  matrix products  21.8 us (6%)
  local copies, waits for them, and re-layouts  16.8 us (5%)
  between operations  14.2 us (4%)
  starting transfers between devices  13.9 us (4%)
    unnamed x2, waiting for transfers between devices  227 us
    ppermute x4, waiting for transfers between devices, passed_along(): lax.ppermute(value, axis, [(source, source + steps) for source in range(i...  21.4 us
    ppermute x4, starting transfers between devices, passed_along(): lax.ppermute(value, axis, [(source, source + steps) for source in range(i...  13.9 us
    unnamed x7, local copies, waits for them, and re-layouts  10.9 us
    sub x1, other arithmetic, shards(): weights = jnp.exp(scores - row_max)  9.99 us
    convert_element_type x1, other arithmetic, shards(): probs_low = probs.astype(jnp.bfloat16)  9.02 us
  transfers between devices with their start and end apart: 5, of which 4 were waited for; matrix products, arithmetic and copies ran while one was open for 2% of the time, Pallas kernels for 0%

commit v1 on v0

--- a/solution.py
+++ b/solution.py
@@ -1,10 +1,19 @@
+import functools
+
 import jax
 import jax.numpy as jnp
 from jax import lax
+from jax.experimental import pallas as pl
+from jax.experimental.pallas import tpu as pltpu
 from jax.sharding import PartitionSpec as P
 
 HEAD_SIZE = 128
 SPAN = 2
+NX, NZ = 4, 8
+NY, NCORE = 4, 2
+GROUPS = 3
+WIDE = 256
+MESH = pl.DeviceIdType.MESH
 
 
 def passed_along(value, axis, steps):
@@ -17,10 +26,298 @@
     return jnp.sum((doc_ends[None, :] <= positions[:, None]).astype(jnp.int32), axis=1)
 
 
-def weight_term(activations, grads):
-    return lax.dot_general(
-        activations, grads, (((0,), (0,)), ((), ())), preferred_element_type=jnp.float32
-    )
+class Place:
+    def __init__(self):
+        self.c = lax.axis_index("ctx")
+        self.t = lax.axis_index("tp")
+        self.x = lax.div(self.c, NZ)
+        self.z = lax.rem(self.c, NZ)
+        self.y = lax.div(self.t, NCORE)
+        self.core = lax.rem(self.t, NCORE)
+
+    def at_x(self, step):
+        return (lax.rem(self.x + step + NX, NX) * NZ + self.z, self.t)
+
+    def at_z(self, step):
+        return (self.x * NZ + lax.rem(self.z + step + NZ, NZ), self.t)
+
+    def at_y(self, step):
+        return (self.c, lax.rem(self.y + step + NY, NY) * NCORE + self.core)
+
+    def sibling(self):
+        return (self.c, self.y * NCORE + 1 - self.core)
+
+    def part(self, ystep, other_core):
+        core = 1 - self.core if other_core else self.core
+        return lax.rem(self.y + ystep + NY, NY) * NCORE + core
+
+
+def remote(src, dst, send, recv, device):
+    return pltpu.make_async_remote_copy(
+        src_ref=src, dst_ref=dst, send_sem=send, recv_sem=recv, device_id=device, device_id_type=MESH
+    )
+
+
+class Acts:
+    def __init__(self, place, act, abuf, local, sends, recvs):
+        self.p, self.act, self.abuf, self.local, self.sends, self.recvs = place, act, abuf, local, sends, recvs
+        self.tokens = act.shape[0]
+        self.share = self.tokens // (NY * NCORE)
+        self.quarter = act.shape[1] // NX
+
+    def rows(self, part):
+        return pl.ds(pl.multiple_of(part * self.share, self.share), self.share)
+
+    def own(self):
+        cols = pl.ds(pl.multiple_of(self.p.x * self.quarter, self.quarter), self.quarter)
+        return pltpu.make_async_copy(self.act.at[:, cols], self.abuf.at[0], self.local)
+
+    def x_copy(self, step):
+        there = lax.rem(self.p.x + step, NX)
+        cols = pl.ds(pl.multiple_of(there * self.quarter, self.quarter), self.quarter)
+        rows = self.rows(self.p.t)
+        return remote(
+            self.act.at[rows, cols],
+            self.abuf.at[step, rows, :],
+            self.sends.at[step - 1],
+            self.recvs.at[step - 1],
+            self.p.at_x(step),
+        )
+
+    def y_copy(self, step):
+        rows = self.rows(self.p.t)
+        piece = self.abuf.at[pl.ds(1, NX - 1), rows, :]
+        return remote(piece, piece, self.sends.at[2 + step], self.recvs.at[2 + step], self.p.at_y(step))
+
+    def y_landed(self, step):
+        rows = self.rows(self.p.part(-step, False))
+        piece = self.abuf.at[pl.ds(1, NX - 1), rows, :]
+        return remote(piece, piece, self.sends.at[2 + step], self.recvs.at[2 + step], self.p.at_y(step))
+
+    def core_copy(self, step):
+        rows = self.rows(self.p.part(-step, False))
+        piece = self.abuf.at[pl.ds(1, NX - 1), rows, :]
+        return remote(piece, piece, self.sends.at[6 + step], self.recvs.at[6 + step], self.p.sibling())
+
+    def start(self):
+        self.own().start()
+        for step in (2, 1, 3):
+            self.x_copy(step).start()
+
+    def spread_y(self):
+        for step in (1, 2, 3):
+            self.x_copy(step).wait_recv()
+        for step in (2, 1, 3):
+            self.y_copy(step).start()
+        self.core_copy(0).start()
+
+    def spread_core(self):
+        for step in (1, 3, 2):
+            self.y_landed(step).wait_recv()
+            self.core_copy(step).start()
+
+    def landed(self):
+        self.own().wait()
+        for step in range(NY):
+            self.core_copy(step).wait_recv()
+
+    def finish(self):
+        for step in (1, 2, 3):
+            self.x_copy(step).wait_send()
+            self.y_copy(step).wait_send()
+        for step in range(NY):
+            self.core_copy(step).wait_send()
+
+
+class Gather:
+    def __init__(self, place, gbuf, sends, recvs):
+        self.p, self.gbuf, self.sends, self.recvs = place, gbuf, sends, recvs
+
+    def copy(self, group, way):
+        whole = pl.ds(group * WIDE, WIDE)
+        half = WIDE // 2
+        source, target, rows, step = (
+            (0, 1, whole, 1),
+            (0, 3, whole, -1),
+            (1, 2, pl.ds(group * WIDE, half), 1),
+            (3, 2, pl.ds(group * WIDE + half, half), -1),
+        )[way]
+        return remote(
+            self.gbuf.at[source, rows, :],
+            self.gbuf.at[target, rows, :],
+            self.sends.at[group, way],
+            self.recvs.at[group, way],
+            self.p.at_x(step),
+        )
+
+    def start(self, group):
+        self.copy(group, 0).start()
+        self.copy(group, 1).start()
+
+    def forward(self, group):
+        self.copy(group, 0).wait_recv()
+        self.copy(group, 2).start()
+        self.copy(group, 1).wait_recv()
+        self.copy(group, 3).start()
+
+    def landed(self, group):
+        self.copy(group, 2).wait_recv()
+        self.copy(group, 3).wait_recv()
+
+    def finish(self, group):
+        for way in range(4):
+            self.copy(group, way).wait_send()
+
+
+class Scatter:
+    def __init__(self, place, terms, sbuf, rbuf, sends, recvs):
+        self.p, self.terms, self.sbuf, self.rbuf, self.sends, self.recvs = place, terms, sbuf, rbuf, sends, recvs
+
+    def rows(self, way, step):
+        if step:
+            return slice(0, WIDE)
+        return slice(way * (WIDE // 2), (way + 1) * (WIDE // 2))
+
+    def copy(self, group, way, step):
+        rows = self.rows(way, step)
+        return remote(
+            self.sbuf.at[group, way, step, rows, :],
+            self.rbuf.at[group, way, step, rows, :],
+            self.sends.at[group, way, step],
+            self.recvs.at[group, way, step],
+            self.p.at_z(1 - 2 * way),
+        )
+
+    def step(self, group, step):
+        for way in range(2):
+            owner = lax.rem(self.p.z + (1 - 2 * way) * (NZ // 2 - step) + NZ, NZ)
+            if step:
+                self.copy(group, way, step - 1).wait_recv()
+            for half in range(2):
+                rows = slice(half * (WIDE // 2), (half + 1) * (WIDE // 2))
+                if step == 0 and half != way:
+                    continue
+                total = self.terms[group, owner, rows, :]
+                if step > 1 or (step == 1 and half == way):
+                    total += self.rbuf[group, way, step - 1, rows, :].astype(jnp.float32)
+                self.sbuf[group, way, step, rows, :] = total.astype(jnp.bfloat16)
+            self.copy(group, way, step).start()
+
+    def result(self, group):
+        last = NZ // 2 - 1
+        total = self.terms[group, self.p.z]
+        for way in range(2):
+            self.copy(group, way, last).wait_recv()
+            total += self.rbuf[group, way, last].astype(jnp.float32)
+        return total.T.astype(jnp.bfloat16)
+
+    def finish(self, group):
+        for way in range(2):
+            for step in range(NZ // 2):
+                self.copy(group, way, step).wait_send()
+
+
+def weight_terms(group, abuf, gbuf, terms):
+    rows = pl.ds(group * WIDE, WIDE)
+    width = terms.shape[3]
+    per = WIDE // width
+
+    def columns(n, carry):
+        cols = pl.ds(pl.multiple_of(n * WIDE, WIDE), WIDE)
+        total = None
+        for slot in range(NX):
+            term = jnp.dot(gbuf[slot, rows, :], abuf[slot, :, cols], preferred_element_type=jnp.float32)
+            total = term if total is None else total + term
+        for k in range(per):
+            terms[group, n * per + k] = total[:, k * width : (k + 1) * width]
+        return carry
+
+    lax.fori_loop(0, NZ // per, columns, 0)
+
+
+def greet(place):
+    barrier = pltpu.get_barrier_semaphore()
+    others = [place.at_x(s) for s in (1, 2, 3)] + [place.at_y(s) for s in (1, 2, 3)]
+    others += [place.sibling(), place.at_z(1), place.at_z(-1)]
+    for other in others:
+        pl.semaphore_signal(barrier, inc=1, device_id=other, device_id_type=MESH)
+    pl.semaphore_wait(barrier, len(others))
+
+
+def weights_kernel(
+    act, grads, wq, wk, wv, abuf, gbuf, terms, sbuf, rbuf, local, own_sem, as_, ar_, gs_, gr_, ss_, sr_
+):
+    place = Place()
+    acts = Acts(place, act, abuf, local, as_, ar_)
+    gather = Gather(place, gbuf, gs_, gr_)
+    scatter = Scatter(place, terms, sbuf, rbuf, ss_, sr_)
+    own = pltpu.make_async_copy(grads, gbuf.at[0], own_sem)
+    own.start()
+    greet(place)
+    acts.start()
+    own.wait()
+    for group in range(GROUPS):
+        gather.start(group)
+    acts.spread_y()
+    gather.forward(0)
+    gather.forward(1)
+    acts.spread_core()
+    gather.forward(2)
+    acts.landed()
+    order = [(0, 0)], [(0, 1), (1, 0)], [(0, 2), (1, 1), (2, 0)]
+    for group in range(GROUPS):
+        gather.landed(group)
+        weight_terms(group, abuf, gbuf, terms)
+        for which, step in order[group]:
+            scatter.step(which, step)
+    for which, step in [(0, 3), (1, 2), (2, 1), (1, 3), (2, 2)]:
+        scatter.step(which, step)
+    wq[:, 0:WIDE] = scatter.result(0)
+    scatter.step(2, 3)
+    wq[:, WIDE : 2 * WIDE] = scatter.result(1)
+    both = scatter.result(2)
+    wk[...] = both[:, 0:HEAD_SIZE]
+    wv[...] = both[:, HEAD_SIZE:WIDE]
+    acts.finish()
+    for group in range(GROUPS):
+        gather.finish(group)
+        scatter.finish(group)
+
+
+def weight_grads(activations, grads):
+    tokens, features = activations.shape
+    quarter = features // NX
+    chunk = quarter // NZ
+    bf16, f32 = jnp.bfloat16, jnp.float32
+    dma = pltpu.SemaphoreType.DMA
+    return pl.pallas_call(
+        weights_kernel,
+        out_shape=(
+            jax.ShapeDtypeStruct((chunk, 2 * WIDE), bf16),
+            jax.ShapeDtypeStruct((chunk, HEAD_SIZE), bf16),
+            jax.ShapeDtypeStruct((chunk, HEAD_SIZE), bf16),
+        ),
+        in_specs=[pl.BlockSpec(memory_space=pl.ANY), pl.BlockSpec(memory_space=pl.ANY)],
+        out_specs=[pl.BlockSpec(memory_space=pltpu.VMEM)] * 3,
+        scratch_shapes=[
+            pltpu.VMEM((NX, tokens, quarter), bf16),
+            pltpu.VMEM((NX, GROUPS * WIDE, tokens), bf16),
+            pltpu.VMEM((GROUPS, NZ, WIDE, chunk), f32),
+            pltpu.VMEM((GROUPS, 2, NZ // 2, WIDE, chunk), bf16),
+            pltpu.VMEM((GROUPS, 2, NZ // 2, WIDE, chunk), bf16),
+            dma,
+            dma,
+            dma((10,)),
+            dma((10,)),
+            dma((GROUPS, 4)),
+            dma((GROUPS, 4)),
+            dma((GROUPS, 2, NZ // 2)),
+            dma((GROUPS, 2, NZ // 2)),
+        ],
+        compiler_params=pltpu.CompilerParams(
+            collective_id=0, has_side_effects=True, vmem_limit_bytes=40 * 2**20
+        ),
+    )(activations, grads)
 
 
 def shards(doc_lengths, activations, queries, key_heads, head_values, output_gradient):
@@ -30,14 +327,15 @@
     group_width = query_group_size * HEAD_SIZE
     att_scale = HEAD_SIZE ** (-0.5)
     first_pos = lax.axis_index("ctx") * tok_rows
-    doc_ends = jnp.cumsum(doc_lengths)
+    docs = jnp.arange(doc_lengths.shape[0])
+    doc_ends = jnp.sum(jnp.where(docs[None, :] <= docs[:, None], doc_lengths[None, :], 0), axis=1)
     query_pos = first_pos + jnp.arange(tok_rows, dtype=jnp.int32)
     key_pos = first_pos - SPAN * tok_rows + jnp.arange((SPAN + 1) * tok_rows, dtype=jnp.int32)
     same_doc = doc_index(doc_ends, query_pos)[:, None] == doc_index(doc_ends, key_pos)[None, :]
     visible = same_doc & (key_pos[None, :] <= query_pos[:, None]) & (key_pos[None, :] >= 0)
     packed = jnp.concatenate([key_heads, head_values], axis=1)
-    remote = [passed_along(packed, "ctx", distance) for distance in range(1, SPAN + 1)]
-    span_rows = jnp.concatenate(remote[::-1] + [packed], axis=0)
+    gone = [passed_along(packed, "ctx", distance) for distance in range(1, SPAN + 1)]
+    span_rows = jnp.concatenate(gone[::-1] + [packed], axis=0)
     key_span_rows = span_rows[:, :key_value_width]
     value_span_rows = span_rows[:, key_value_width:]
     query_group = queries.reshape(tok_rows, query_group_size, HEAD_SIZE)
@@ -71,34 +369,20 @@
     value_grad = jnp.einsum(
         "gtk,tgd->kd", probs_low, grad_group, preferred_element_type=jnp.float32
     )
-    query_parts = query_grad.reshape(tok_rows, group_width)
-    query_low = query_parts.astype(jnp.bfloat16)
+    query_low = query_grad.reshape(tok_rows, group_width).astype(jnp.bfloat16)
     kv_grad = jnp.concatenate([key_grad, value_grad], axis=1)
     far_terms = [
         kv_grad[(SPAN - 1 - offset) * tok_rows : (SPAN - offset) * tok_rows]
         for offset in range(SPAN)
     ]
-    local_part = kv_grad[SPAN * tok_rows :]
-    returned = local_part
+    returned = kv_grad[SPAN * tok_rows :]
     for distance in range(1, SPAN + 1):
         returned = returned + passed_along(
             far_terms[distance - 1].astype(jnp.bfloat16), "ctx", -distance
         ).astype(jnp.float32)
     kv_low = returned.astype(jnp.bfloat16)
     joined = jnp.concatenate([query_low, kv_low], axis=1)
-    all_grads = lax.psum_scatter(
-        weight_term(activations, joined).astype(jnp.bfloat16),
-        "ctx",
-        scatter_dimension=0,
-        tiled=True,
-    )
-    query_weight_grad = all_grads[:, : query_low.shape[1]]
-    kv_weight_grad = all_grads[:, query_low.shape[1] :]
-    return (
-        query_weight_grad,
-        kv_weight_grad[:, :key_value_width],
-        kv_weight_grad[:, key_value_width:],
-    )
+    return weight_grads(activations, joined.T)
 
 
 def solution(mesh):

time: 339 us -> 143 us (0.42)
  waiting for transfers between devices: 248 us -> 20.3 us
  Pallas kernels: 0 us -> 65.7 us
  between operations: 14.2 us -> 0.88 us
  local copies, waits for them, and re-layouts: 16.8 us -> 7.33 us
  matrix products: 21.8 us -> 15.4 us
    unnamed x2 -> x0, waiting for transfers between devices: 227 us -> none
    pallas_call x0 -> x1, Pallas kernels: none -> 65.7 us  [weight_grads(): pl.pallas_call(weights_kernel, out_shape=(jax.ShapeDtypeStruct((chunk, 2...]
    unnamed x7 -> x17, local copies, waits for them, and re-layouts: 10.9 us -> 5.1 us
    dot_general x1 -> x0, matrix products: 5.4 us -> none  [weight_term(): lax.dot_general(activations, grads, (((0,), (0,)), ((), ())), preferred_e...]
  transfers between devices with their start and end apart: 5 -> 4, of which waited for: 4 -> 3; matrix products, arithmetic and copies ran while one was open for 2% -> 6% of each run, Pallas kernels for 0% -> 0%
where the time goes in v1:
time: 143 us; the launch traced here: 142 us
  Pallas kernels  65.7 us (46%)
  waiting for transfers between devices  20.3 us (14%)
  other arithmetic  18.9 us (13%)
  matrix products  15.4 us (11%)
  starting transfers between devices  13.9 us (10%)
  local copies, waits for them, and re-layouts  7.33 us (5%)
    pallas_call x1, Pallas kernels, weight_grads(): pl.pallas_call(weights_kernel, out_shape=(jax.ShapeDtypeStruct((chunk, 2...  65.7 us
    ppermute x4, waiting for transfers between devices, passed_along(): lax.ppermute(value, axis, [(source, source + steps) for source in range(i...  20.3 us
    ppermute x4, starting transfers between devices, passed_along(): lax.ppermute(value, axis, [(source, source + steps) for source in range(i...  13.9 us
    sub x1, other arithmetic, shards(): weights = jnp.exp(scores - row_max)  8.82 us
    convert_element_type x1, other arithmetic, shards(): probs_low = probs.astype(jnp.bfloat16)  6.41 us
    unnamed x17, local copies, waits for them, and re-layouts  5.1 us
    dot_general x1, matrix products, shards(): jnp.einsum('tgd,kd->gtk', grad_group, value_span_rows, preferred_element_...  3.09 us
    dot_general x1, matrix products, shards(): jnp.einsum('gtk,tgd->kd', probs_low, grad_group, preferred_element_type=j...  3.01 us
  transfers between devices with their start and end apart: 4, of which 3 were waited for; matrix products, arithmetic and copies ran while one was open for 6% of the time, Pallas kernels for 0%

profile of v1, /device:TPU:32, one launch (start us, length us, event | category | flops | bytes accessed | tf_op | source)
XLA Modules:
  0.0 142.4 jit_solution(6448647218341092852)
XLA Ops:
  0.6 0.9 constant_dynamic-update-slice_fusion.1
  1.6 0.9 constant_dynamic-update-slice_fusion
  2.5 5.2 %collective-permute-start = (bf16[512,256]{1,0:T(8,128)(2,1)S(1)}, bf16[512,256]{1,0:T(8,128)(2,1)S(1)}, u32[]{:S(2)}, u32[]{:S(2)}) collective-permute-start(bf16[512,256]{1,0:T(8,128)(2,1)S(1)} %constant_dynamic-update-slice_fusion), channel_id=1, source_target_pairs={{0,16},{8,24},{16,32},{24,40},{32,48},{40,56},{48,64},{56,72},{64,... | collective-permute-start | bytes 786440 | tf_op jit(solution)/shard_map/ppermute | solution.py:22
  7.7 5.0 %collective-permute-start.1 = (bf16[512,256]{1,0:T(8,128)(2,1)S(1)}, bf16[512,256]{1,0:T(8,128)(2,1)S(1)}, u32[]{:S(2)}, u32[]{:S(2)}) collective-permute-start(bf16[512,256]{1,0:T(8,128)(2,1)S(1)} %constant_dynamic-update-slice_fusion), channel_id=1, source_target_pairs={{0,8},{8,16},{16,24},{24,32},{32,40},{40,48},{48,56},{56,64},{64,7... | collective-permute-start | bytes 786440 | tf_op jit(solution)/shard_map/ppermute | solution.py:22
  12.8 0.8 select_reduce_fusion
  13.5 0.1 convert_reduce_fusion
  13.7 0.1 convert_reduce_fusion.1
  13.8 1.3 copy.38
  15.0 2.3 %copy.20 = bf16[512,512]{0,1:T(8,128)(2,1)} copy(bf16[512,512]{1,0:T(8,128)(2,1)} %param.11) | data formatting | bytes 1048576 | tf_op args[5]
  17.3 1.5 %and_and_fusion = pred[512,1536]{0,1:T(8,128)(4,1)S(1)} fusion(s32[512]{0:T(512)S(1)} %iota_add_fusion.1, s32[512]{0:T(512)S(1)} %convert_reduce_fusion.1, s32[1536]{0:T(1024)S(1)} %iota_add_fusion, s32[1536]{0:T(1024)S(1)} %convert_reduce_fusion, pred[1536]{0:T(1024)(128)(4,1)S(1)} %broadcast_compare_fusion), kind=kLoop, calls=%fused_computation.12 | loop fusion | flops 3145728 | bytes 804352 | tf_op jit(solution)/shard_map/and | solution.py:335
  18.8 6.3 %collective-permute-done.1 = bf16[512,256]{1,0:T(8,128)(2,1)S(1)} collective-permute-done((bf16[512,256]{1,0:T(8,128)(2,1)S(1)}, bf16[512,256]{1,0:T(8,128)(2,1)S(1)}, u32[]{:S(2)}, u32[]{:S(2)}) %collective-permute-start.1) | collective-permute-done | bytes 262176 | tf_op jit(solution)/shard_map/ppermute | solution.py:22
  25.1 1.0 pad_maximum_fusion.1
  26.1 2.8 %fusion.16 = f32[1536,512,4]{1,0,2:T(8,128)S(1)} fusion(bf16[512,4,128]{0,2,1:T(8,128)(2,1)S(1)} %bitcast.51, bf16[1536,256]{1,0:T(8,128)(2,1)} %pad_maximum_fusion.1), kind=kOutput, calls=%fused_computation.32 | convolution fusion | flops 805306368 | bytes 13500416 | tf_op jit(solution)/shard_map/tgd,kd->gtk/dot_general | solution.py:344
  28.9 8.8 %fusion.20 = (f32[4,512]{1,0:T(4,128)S(1)}, f32[4,512,1536]{1,2,0:T(8,128)}) fusion(f32[1536,512,4]{1,0,2:T(8,128)S(1)} %fusion.16, pred[512,1536]{0,1:T(8,128)(4,1)S(1)} %and_and_fusion), kind=kOutput, calls=%fused_computation.45 | output fusion | flops 18875904 | bytes 25960448 | tf_op jit(solution)/shard_map/sub | solution.py:349
  37.7 6.4 %fusion.7 = bf16[4,512,1536]{1,2,0:T(8,128)(2,1)S(1)} fusion(f32[4,512,1536]{1,2,0:T(8,128)} %get-tuple-element.6, f32[4,512]{1,0:T(4,128)S(1)} %get-tuple-element.5), kind=kLoop, calls=%fused_computation.11 | loop fusion | flops 6291456 | bytes 18882560 | tf_op jit(solution)/shard_map/convert_element_type | solution.py:351
  44.1 2.4 %fusion.11 = f32[4,512]{1,0:T(4,128)S(1)} fusion(bf16[4,512,1536]{1,2,0:T(8,128)(2,1)S(1)} %fusion.7, bf16[512,4,128]{0,2,1:T(8,128)(2,1)} %bitcast.53, bf16[1536,256]{1,0:T(8,128)(2,1)} %pad_maximum_fusion.1), kind=kOutput, calls=%fused_computation.23 | convolution fusion | flops 806090752 | bytes 7217152 | tf_op jit(solution)/shard_map/gtk,kd->gtd/dot_general | solution.py:352
  46.5 3.0 %convolution_bitcast_fusion = f32[1536,128]{0,1:T(8,128)} fusion(bf16[4,512,1536]{1,2,0:T(8,128)(2,1)S(1)} %fusion.7, bf16[512,4,128]{0,2,1:T(8,128)(2,1)S(1)} %bitcast.55), kind=kOutput, calls=%fused_computation.13 | convolution fusion | flops 805306368 | bytes 7602176 | tf_op jit(solution)/shard_map/gtk,tgd->kd/dot_general | solution.py:369
  49.5 3.1 %fusion.2 = bf16[4,512,1536]{1,2,0:T(8,128)(2,1)S(1)} fusion(bf16[512,4,128]{0,2,1:T(8,128)(2,1)} %bitcast.54, f32[4,512]{1,0:T(4,128)S(1)} %fusion.11, f32[4,512,1536]{1,2,0:T(8,128)S(1)} %copy-done.1, f32[4,512]{1,0:T(4,128)S(1)} %get-tuple-element.5, bf16[1536,256]{1,0:T(8,128)(2,1)} %pad_maximum_fusion.1), kind=kOutput, calls=%fused_computation.3 | convolution fusion | flops 817889280 | bytes 19808256 | tf_op jit(solution)/shard_map/tgd,kd->gtk/dot_general | solution.py:356
  52.6 2.1 %fusion.8 = f32[1536,128]{0,1:T(8,128)S(1)} fusion(bf16[4,512,1536]{1,2,0:T(8,128)(2,1)S(1)} %fusion.2, bf16[512,4,128]{0,2,1:T(8,128)(2,1)S(1)} %bitcast.52), kind=kOutput, calls=%fused_computation.15 | convolution fusion | flops 805502976 | bytes 7602176 | tf_op jit(solution)/shard_map/gtk,tgd->kd/dot_general | solution.py:366
  54.8 0.1 fusion.9
  54.9 0.0 copy-start
  54.9 2.2 %collective-permute-start.2 = (bf16[512,256]{0,1:T(8,128)(2,1)S(1)}, bf16[512,256]{0,1:T(8,128)(2,1)S(1)}, u32[]{:S(2)}, u32[]{:S(2)}) collective-permute-start(bf16[512,256]{0,1:T(8,128)(2,1)S(1)} %get-tuple-element.3), channel_id=1, source_target_pairs={{8,0},{16,8},{24,16},{32,24},{40,32},{48,40},{56,48},{64,56},{72,6... | collective-permute-start | bytes 786440 | tf_op jit(solution)/shard_map/ppermute | solution.py:22
  57.1 1.5 %collective-permute-start.3 = (bf16[512,256]{0,1:T(8,128)(2,1)S(1)}, bf16[512,256]{0,1:T(8,128)(2,1)S(1)}, u32[]{:S(2)}, u32[]{:S(2)}) collective-permute-start(bf16[512,256]{0,1:T(8,128)(2,1)S(1)} %get-tuple-element.4), channel_id=1, source_target_pairs={{16,0},{24,8},{32,16},{40,24},{48,32},{56,40},{64,48},{72,56},{80,... | collective-permute-start | bytes 786440 | tf_op jit(solution)/shard_map/ppermute | solution.py:22
  58.6 2.0 %fusion.10 = bf16[128,4,512]{2,0,1:T(8,128)(2,1)S(1)} fusion(bf16[4,512,1536]{1,2,0:T(8,128)(2,1)S(1)} %fusion.2, bf16[1536,256]{1,0:T(8,128)(2,1)} %pad_maximum_fusion.1), kind=kOutput, calls=%fused_computation.22 | convolution fusion | flops 805830656 | bytes 7208960 | tf_op jit(solution)/shard_map/gtk,kd->tgd/dot_general | solution.py:362
  60.7 6.4 %collective-permute-done.2 = bf16[512,256]{0,1:T(8,128)(2,1)S(1)} collective-permute-done((bf16[512,256]{0,1:T(8,128)(2,1)S(1)}, bf16[512,256]{0,1:T(8,128)(2,1)S(1)}, u32[]{:S(2)}, u32[]{:S(2)}) %collective-permute-start.2) | collective-permute-done | bytes 262176 | tf_op jit(solution)/shard_map/ppermute | solution.py:22
  67.1 7.6 %collective-permute-done.3 = bf16[512,256]{0,1:T(8,128)(2,1)S(1)} collective-permute-done((bf16[512,256]{0,1:T(8,128)(2,1)S(1)}, bf16[512,256]{0,1:T(8,128)(2,1)S(1)}, u32[]{:S(2)}, u32[]{:S(2)}) %collective-permute-start.3) | collective-permute-done | bytes 262176 | tf_op jit(solution)/shard_map/ppermute | solution.py:22
  74.7 0.1 fusion.15
  74.8 0.1 maximum_bitcast_fusion.grads
  74.8 65.7 %shard_map.85 = (bf16[128,512]{1,0:T(8,128)(2,1)S(1)}, bf16[128,128]{1,0:T(8,128)(2,1)S(1)}, bf16[128,128]{1,0:T(8,128)(2,1)S(1)}) custom-call(bf16[512,4096]{1,0:T(8,128)(2,1)S(1)} %copy-done, bf16[768,512]{1,0:T(8,128)(2,1)S(1)} %maximum_bitcast_fusion.grads), custom_call_target="tpu_custom_call" | custom-call | tf_op jit(solution)/shard_map/pallas_call | solution.py:293
  140.5 0.7 copy.43
  141.2 0.6 copy.44
  141.8 0.6 copy.45
  (16 shorter events, 0.1 us)
Async XLA Ops:
  2.5 16.3 %collective-permute-start = (bf16[512,256]{1,0:T(8,128)(2,1)S(1)}, bf16[512,256]{1,0:T(8,128)(2,1)S(1)}, u32[]{:S(2)}, u32[]{:S(2)}) collective-permute-start(bf16[512,256]{1,0:T(8,128)(2,1)S(1)} %constant_dynamic-update-slice_fusion), channel_id=1, source_target_pairs={{0,16},{8,24},{16,32},{24,40},{32,48},{40,56},{48,64},{56,72},{64,... | collective-permute-start | bytes 786440 | tf_op jit(solution)/shard_map/ppermute | solution.py:22
  7.7 17.4 %collective-permute-start.1 = (bf16[512,256]{1,0:T(8,128)(2,1)S(1)}, bf16[512,256]{1,0:T(8,128)(2,1)S(1)}, u32[]{:S(2)}, u32[]{:S(2)}) collective-permute-start(bf16[512,256]{1,0:T(8,128)(2,1)S(1)} %constant_dynamic-update-slice_fusion), channel_id=1, source_target_pairs={{0,8},{8,16},{16,24},{24,32},{32,40},{40,48},{48,56},{56,64},{64,7... | collective-permute-start | bytes 786440 | tf_op jit(solution)/shard_map/ppermute | solution.py:22
  15.0 13.8 %copy-start.3 = (bf16[512,512]{0,1:T(8,128)(2,1)}, bf16[512,512]{0,1:T(8,128)(2,1)S(1)}, u32[]{:S(2)}) copy-start(bf16[512,512]{0,1:T(8,128)(2,1)S(1)} %copy.38) | copy-start | bytes 1572868
  44.1 2.4 %copy-start.5 = (bf16[512,512]{0,1:T(8,128)(2,1)S(1)}, bf16[512,512]{0,1:T(8,128)(2,1)}, u32[]{:S(2)}) copy-start(bf16[512,512]{0,1:T(8,128)(2,1)} %copy.20) | copy-start | bytes 1572868
  44.1 5.4 %copy-start.1 = (f32[4,512,1536]{1,2,0:T(8,128)S(1)}, f32[4,512,1536]{1,2,0:T(8,128)}, u32[]{:S(2)}) copy-start(f32[4,512,1536]{1,2,0:T(8,128)} %get-tuple-element.6) | copy-start | bytes 37748740
  49.5 3.1 %copy-start.4 = (bf16[512,512]{0,1:T(8,128)(2,1)S(1)}, bf16[512,512]{0,1:T(8,128)(2,1)}, u32[]{:S(2)}) copy-start(bf16[512,512]{0,1:T(8,128)(2,1)} %copy-done.3) | copy-start | bytes 1572868
  52.6 2.2 %copy-start.2 = (f32[1536,128]{0,1:T(8,128)S(1)}, f32[1536,128]{0,1:T(8,128)}, u32[]{:S(2)}) copy-start(f32[1536,128]{0,1:T(8,128)} %convolution_bitcast_fusion) | copy-start | bytes 2359300
  54.9 20.0 %copy-start = (bf16[512,4096]{1,0:T(8,128)(2,1)S(1)}, bf16[512,4096]{1,0:T(8,128)(2,1)}, u32[]{:S(2)}) copy-start(bf16[512,4096]{1,0:T(8,128)(2,1)} %act.1) | copy-start | bytes 12582916
  54.9 12.1 %collective-permute-start.2 = (bf16[512,256]{0,1:T(8,128)(2,1)S(1)}, bf16[512,256]{0,1:T(8,128)(2,1)S(1)}, u32[]{:S(2)}, u32[]{:S(2)}) collective-permute-start(bf16[512,256]{0,1:T(8,128)(2,1)S(1)} %get-tuple-element.3), channel_id=1, source_target_pairs={{8,0},{16,8},{24,16},{32,24},{40,32},{48,40},{56,48},{64,56},{72,6... | collective-permute-start | bytes 786440 | tf_op jit(solution)/shard_map/ppermute | solution.py:22
  57.1 17.5 %collective-permute-start.3 = (bf16[512,256]{0,1:T(8,128)(2,1)S(1)}, bf16[512,256]{0,1:T(8,128)(2,1)S(1)}, u32[]{:S(2)}, u32[]{:S(2)}) collective-permute-start(bf16[512,256]{0,1:T(8,128)(2,1)S(1)} %get-tuple-element.4), channel_id=1, source_target_pairs={{16,0},{24,8},{32,16},{40,24},{48,32},{56,40},{64,48},{72,56},{80,... | collective-permute-start | bytes 786440 | tf_op jit(solution)/shard_map/ppermute | solution.py:22

commit v2 on v1

--- a/solution.py
+++ b/solution.py
@@ -1,4 +1,4 @@
-import functools
+import math
 
 import jax
 import jax.numpy as jnp
@@ -13,17 +13,8 @@
 NY, NCORE = 4, 2
 GROUPS = 3
 WIDE = 256
+REACH = 5
 MESH = pl.DeviceIdType.MESH
-
-
-def passed_along(value, axis, steps):
-    count = lax.axis_size(axis)
-    initial, last = (max(0, -steps), min(count, count - steps))
-    return lax.ppermute(value, axis, [(source, source + steps) for source in range(initial, last)])
-
-
-def doc_index(doc_ends, positions):
-    return jnp.sum((doc_ends[None, :] <= positions[:, None]).astype(jnp.int32), axis=1)
 
 
 class Place:
@@ -43,6 +34,10 @@
 
     def at_y(self, step):
         return (self.c, lax.rem(self.y + step + NY, NY) * NCORE + self.core)
+
+    def at_c(self, step):
+        count = NX * NZ
+        return (lax.rem(self.c + step + count, count), self.t)
 
     def sibling(self):
         return (self.c, self.y * NCORE + 1 - self.core)
@@ -134,13 +129,15 @@
         self.p, self.gbuf, self.sends, self.recvs = place, gbuf, sends, recvs
 
     def copy(self, group, way):
-        whole = pl.ds(group * WIDE, WIDE)
-        half = WIDE // 2
+        whole = pl.ds(pl.multiple_of(group * HEAD_SIZE, HEAD_SIZE), HEAD_SIZE)
+        half = HEAD_SIZE // 2
+        lower = pl.ds(pl.multiple_of(group * HEAD_SIZE, half), half)
+        upper = pl.ds(pl.multiple_of(group * HEAD_SIZE + half, half), half)
         source, target, rows, step = (
             (0, 1, whole, 1),
             (0, 3, whole, -1),
-            (1, 2, pl.ds(group * WIDE, half), 1),
-            (3, 2, pl.ds(group * WIDE + half, half), -1),
+            (1, 2, lower, 1),
+            (3, 2, upper, -1),
         )[way]
         return remote(
             self.gbuf.at[source, rows, :],
@@ -235,154 +232,284 @@
     lax.fori_loop(0, NZ // per, columns, 0)
 
 
+class Span:
+    def __init__(self, place, kbuf, vbuf, sends, recvs):
+        self.p, self.bufs, self.sends, self.recvs = place, (kbuf, vbuf), sends, recvs
+
+    def copy(self, which, hop):
+        buf = self.bufs[which]
+        source, target = (pl.ds(4, 2), pl.ds(2, 2)) if hop == 0 else (pl.ds(2, 2), pl.ds(0, 2))
+        return remote(
+            buf.at[source], buf.at[target], self.sends.at[which, hop], self.recvs.at[which, hop], self.p.at_c(1)
+        )
+
+    def finish(self):
+        for which in range(2):
+            for hop in range(2):
+                self.copy(which, hop).wait_send()
+
+
+class Return:
+    def __init__(self, place, accs, sbuf, rbuf, sends, recvs):
+        self.p, self.accs, self.sbuf, self.rbuf, self.sends, self.recvs = place, accs, sbuf, rbuf, sends, recvs
+
+    def copy(self, which, hop):
+        return remote(
+            self.sbuf.at[which, hop],
+            self.rbuf.at[which, hop],
+            self.sends.at[which, hop],
+            self.recvs.at[which, hop],
+            self.p.at_c(-1),
+        )
+
+    def start(self, which, hop):
+        if hop:
+            self.copy(which, 0).wait_recv()
+        for k in range(2):
+            total = self.accs[which][2 * hop + k]
+            if hop:
+                total += self.rbuf[which, 0, k].astype(jnp.float32)
+            self.sbuf[which, hop, k] = total.astype(jnp.bfloat16)
+        self.copy(which, hop).start()
+
+    def landed(self, which, factor, gbuf, row):
+        self.copy(which, 1).wait_recv()
+        for k in range(2):
+            total = self.accs[which][4 + k] + self.rbuf[which, 1, k].astype(jnp.float32)
+            gbuf[0, row : row + HEAD_SIZE, k * WIDE : (k + 1) * WIDE] = (total * factor).astype(jnp.bfloat16).T
+
+    def finish(self):
+        for which in range(2):
+            for hop in range(2):
+                self.copy(which, hop).wait_send()
+
+
 def greet(place):
     barrier = pltpu.get_barrier_semaphore()
     others = [place.at_x(s) for s in (1, 2, 3)] + [place.at_y(s) for s in (1, 2, 3)]
-    others += [place.sibling(), place.at_z(1), place.at_z(-1)]
+    others += [place.sibling(), place.at_z(1), place.at_z(-1), place.at_c(1), place.at_c(-1)]
     for other in others:
         pl.semaphore_signal(barrier, inc=1, device_id=other, device_id_type=MESH)
     pl.semaphore_wait(barrier, len(others))
 
 
-def weights_kernel(
-    act, grads, wq, wk, wv, abuf, gbuf, terms, sbuf, rbuf, local, own_sem, as_, ar_, gs_, gr_, ss_, sr_
+def doc_starts(docs, first, out):
+    pos = first + lax.broadcasted_iota(jnp.int32, (1, out.shape[1]), 1)
+    start = jnp.zeros_like(pos)
+    end = jnp.int32(0)
+    for n in range(docs.shape[0]):
+        end = end + docs[n]
+        start = jnp.where(pos >= end, end, start)
+    out[...] = start
+
+
+def attend(h, first, starts, kbuf, vbuf, kt, qh, gh, qt, gt, sc, dp, dk, dv, gbuf):
+    f32, bf16 = jnp.float32, jnp.bfloat16
+    scale = HEAD_SIZE**-0.5
+    factor = scale * math.log2(math.e)
+    near = lambda qs: slice(qs * WIDE, (qs + 1) * WIDE)
+    row = lax.broadcasted_iota(jnp.int32, (WIDE, WIDE), 0)
+    col = lax.broadcasted_iota(jnp.int32, (WIDE, WIDE), 1)
+    base = first - 2 * qh.shape[1]
+    tops, sums, deltas = [], [], []
+    for qs in range(2):
+        begin = starts[:, near(qs)] - base
+        top = None
+        for j in range(REACH):
+            s = jnp.dot(kbuf[qs + j], qt[h, :, near(qs)], preferred_element_type=f32)
+            seen = row >= begin - (qs + j) * WIDE
+            if j == REACH - 1:
+                seen &= row <= col
+            s = jnp.where(seen, s, -jnp.inf)
+            sc[qs, j] = s
+            most = jnp.max(s, axis=0, keepdims=True)
+            top = most if top is None else jnp.maximum(top, most)
+        tops.append(top)
+    for qs in range(2):
+        shift = tops[qs] * factor
+        total = mixed = None
+        for j in range(REACH):
+            p = jnp.exp2(sc[qs, j] * factor - shift)
+            d = jnp.dot(vbuf[qs + j], gt[h, :, near(qs)], preferred_element_type=f32)
+            sc[qs, j] = p
+            dp[qs, j] = d
+            a, b = jnp.sum(p, axis=0, keepdims=True), jnp.sum(p * d, axis=0, keepdims=True)
+            total = a if total is None else total + a
+            mixed = b if mixed is None else mixed + b
+        inverse = 1.0 / total
+        sums.append(inverse)
+        deltas.append(mixed * inverse)
+    for qs in range(2):
+        dq = None
+        for j in range(REACH):
+            p = sc[qs, j] * sums[qs]
+            ds = (p * (dp[qs, j] - deltas[qs])).astype(bf16)
+            dv[qs + j] += jnp.dot(p.astype(bf16), gh[h, near(qs)], preferred_element_type=f32)
+            dk[qs + j] += jnp.dot(ds, qh[h, near(qs)], preferred_element_type=f32)
+            term = jnp.dot(kt[qs + j], ds, preferred_element_type=f32)
+            dq = term if dq is None else dq + term
+        gbuf[0, pl.ds(pl.multiple_of(h * HEAD_SIZE, HEAD_SIZE), HEAD_SIZE), near(qs)] = (dq * scale).astype(bf16)
+
+
+def kernel(
+    docs, act, q, k, v, g, wq, wk, wv,
+    abuf, gbuf, terms, sbuf, rbuf, kbuf, vbuf, kt, qh, gh, qt, gt, sc, dp, dk, dv, starts, back_s, back_r,
+    local, as_, ar_, gs_, gr_, ss_, sr_, ks_, kr_, bs_, br_,
 ):
     place = Place()
     acts = Acts(place, act, abuf, local, as_, ar_)
     gather = Gather(place, gbuf, gs_, gr_)
     scatter = Scatter(place, terms, sbuf, rbuf, ss_, sr_)
-    own = pltpu.make_async_copy(grads, gbuf.at[0], own_sem)
-    own.start()
+    span = Span(place, kbuf, vbuf, ks_, kr_)
+    back = Return(place, (dk, dv), back_s, back_r, bs_, br_)
+    heads = qh.shape[0]
+    tokens = qh.shape[1]
+    first = place.c * tokens
+    for n in range(2):
+        kbuf[4 + n] = k[n * WIDE : (n + 1) * WIDE, :]
+        vbuf[4 + n] = v[n * WIDE : (n + 1) * WIDE, :]
     greet(place)
+    span.copy(0, 0).start()
+    span.copy(1, 0).start()
     acts.start()
-    own.wait()
-    for group in range(GROUPS):
-        gather.start(group)
+    doc_starts(docs, first, starts)
+    dk[...] = jnp.zeros_like(dk)
+    dv[...] = jnp.zeros_like(dv)
+    for h in range(heads):
+        cols = slice(h * HEAD_SIZE, (h + 1) * HEAD_SIZE)
+        qh[h] = q[:, cols]
+        gh[h] = g[:, cols]
+        qt[h] = q[:, cols].T
+        gt[h] = g[:, cols].T
+    for n in (4, 5):
+        kt[n] = kbuf[n].T
+    for which in range(2):
+        span.copy(which, 0).wait_recv()
+        span.copy(which, 1).start()
+    for n in (2, 3):
+        kt[n] = kbuf[n].T
     acts.spread_y()
-    gather.forward(0)
-    gather.forward(1)
-    acts.spread_core()
-    gather.forward(2)
+    span.copy(0, 1).wait_recv()
+    for n in (0, 1):
+        kt[n] = kbuf[n].T
+    span.copy(1, 1).wait_recv()
+
+    def head(h, carry):
+        attend(h, first, starts, kbuf, vbuf, kt, qh, gh, qt, gt, sc, dp, dk, dv, gbuf)
+        gather.start(h)
+
+        @pl.when(h == 0)
+        def _():
+            acts.spread_core()
+
+        @pl.when(h > 0)
+        def _():
+            gather.forward(h - 1)
+
+        return carry
+
+    lax.fori_loop(0, heads, head, 0)
+    back.start(0, 0)
+    back.start(1, 0)
+    gather.forward(3)
     acts.landed()
-    order = [(0, 0)], [(0, 1), (1, 0)], [(0, 2), (1, 1), (2, 0)]
-    for group in range(GROUPS):
-        gather.landed(group)
-        weight_terms(group, abuf, gbuf, terms)
-        for which, step in order[group]:
-            scatter.step(which, step)
-    for which, step in [(0, 3), (1, 2), (2, 1), (1, 3), (2, 2)]:
-        scatter.step(which, step)
+    gather.landed(0)
+    gather.landed(1)
+    weight_terms(0, abuf, gbuf, terms)
+    scatter.step(0, 0)
+    back.start(0, 1)
+    back.start(1, 1)
+    gather.landed(2)
+    gather.landed(3)
+    weight_terms(1, abuf, gbuf, terms)
+    scatter.step(1, 0)
+    scatter.step(0, 1)
+    back.landed(0, HEAD_SIZE**-0.5, gbuf, 4 * HEAD_SIZE)
+    gather.start(4)
+    back.landed(1, 1.0, gbuf, 5 * HEAD_SIZE)
+    gather.start(5)
+    scatter.step(1, 1)
+    scatter.step(0, 2)
+    gather.forward(4)
+    gather.forward(5)
+    scatter.step(1, 2)
+    scatter.step(0, 3)
+    gather.landed(4)
+    gather.landed(5)
+    weight_terms(2, abuf, gbuf, terms)
+    scatter.step(2, 0)
+    scatter.step(1, 3)
     wq[:, 0:WIDE] = scatter.result(0)
+    scatter.step(2, 1)
+    wq[:, WIDE : 2 * WIDE] = scatter.result(1)
+    scatter.step(2, 2)
     scatter.step(2, 3)
-    wq[:, WIDE : 2 * WIDE] = scatter.result(1)
     both = scatter.result(2)
     wk[...] = both[:, 0:HEAD_SIZE]
     wv[...] = both[:, HEAD_SIZE:WIDE]
     acts.finish()
+    span.finish()
+    back.finish()
+    for n in range(heads + 2):
+        gather.finish(n)
     for group in range(GROUPS):
-        gather.finish(group)
         scatter.finish(group)
 
 
-def weight_grads(activations, grads):
+def shards(doc_lengths, activations, queries, key_heads, head_values, output_gradient):
     tokens, features = activations.shape
+    heads = queries.shape[1] // HEAD_SIZE
     quarter = features // NX
     chunk = quarter // NZ
+    blocks = (SPAN + 1) * tokens // WIDE
     bf16, f32 = jnp.bfloat16, jnp.float32
     dma = pltpu.SemaphoreType.DMA
+    vmem = pl.BlockSpec(memory_space=pltpu.VMEM)
     return pl.pallas_call(
-        weights_kernel,
+        kernel,
         out_shape=(
-            jax.ShapeDtypeStruct((chunk, 2 * WIDE), bf16),
+            jax.ShapeDtypeStruct((chunk, heads * HEAD_SIZE), bf16),
             jax.ShapeDtypeStruct((chunk, HEAD_SIZE), bf16),
             jax.ShapeDtypeStruct((chunk, HEAD_SIZE), bf16),
         ),
-        in_specs=[pl.BlockSpec(memory_space=pl.ANY), pl.BlockSpec(memory_space=pl.ANY)],
-        out_specs=[pl.BlockSpec(memory_space=pltpu.VMEM)] * 3,
+        in_specs=[pl.BlockSpec(memory_space=pltpu.SMEM), pl.BlockSpec(memory_space=pl.ANY), vmem, vmem, vmem, vmem],
+        out_specs=[vmem] * 3,
         scratch_shapes=[
             pltpu.VMEM((NX, tokens, quarter), bf16),
             pltpu.VMEM((NX, GROUPS * WIDE, tokens), bf16),
             pltpu.VMEM((GROUPS, NZ, WIDE, chunk), f32),
             pltpu.VMEM((GROUPS, 2, NZ // 2, WIDE, chunk), bf16),
             pltpu.VMEM((GROUPS, 2, NZ // 2, WIDE, chunk), bf16),
-            dma,
+            pltpu.VMEM((blocks, WIDE, HEAD_SIZE), bf16),
+            pltpu.VMEM((blocks, WIDE, HEAD_SIZE), bf16),
+            pltpu.VMEM((blocks, HEAD_SIZE, WIDE), bf16),
+            pltpu.VMEM((heads, tokens, HEAD_SIZE), bf16),
+            pltpu.VMEM((heads, tokens, HEAD_SIZE), bf16),
+            pltpu.VMEM((heads, HEAD_SIZE, tokens), bf16),
+            pltpu.VMEM((heads, HEAD_SIZE, tokens), bf16),
+            pltpu.VMEM((2, REACH, WIDE, WIDE), f32),
+            pltpu.VMEM((2, REACH, WIDE, WIDE), f32),
+            pltpu.VMEM((blocks, WIDE, HEAD_SIZE), f32),
+            pltpu.VMEM((blocks, WIDE, HEAD_SIZE), f32),
+            pltpu.VMEM((1, tokens), jnp.int32),
+            pltpu.VMEM((2, 2, 2, WIDE, HEAD_SIZE), bf16),
+            pltpu.VMEM((2, 2, 2, WIDE, HEAD_SIZE), bf16),
             dma,
             dma((10,)),
             dma((10,)),
-            dma((GROUPS, 4)),
-            dma((GROUPS, 4)),
+            dma((heads + 2, 4)),
+            dma((heads + 2, 4)),
             dma((GROUPS, 2, NZ // 2)),
             dma((GROUPS, 2, NZ // 2)),
+            dma((2, 2)),
+            dma((2, 2)),
+            dma((2, 2)),
+            dma((2, 2)),
         ],
         compiler_params=pltpu.CompilerParams(
-            collective_id=0, has_side_effects=True, vmem_limit_bytes=40 * 2**20
+            collective_id=0, has_side_effects=True, vmem_limit_bytes=48 * 2**20
         ),
-    )(activations, grads)
-
-
-def shards(doc_lengths, activations, queries, key_heads, head_values, output_gradient):
-    tok_rows = key_heads.shape[0]
-    key_value_width = key_heads.shape[1]
-    query_group_size = queries.shape[1] // key_value_width
-    group_width = query_group_size * HEAD_SIZE
-    att_scale = HEAD_SIZE ** (-0.5)
-    first_pos = lax.axis_index("ctx") * tok_rows
-    docs = jnp.arange(doc_lengths.shape[0])
-    doc_ends = jnp.sum(jnp.where(docs[None, :] <= docs[:, None], doc_lengths[None, :], 0), axis=1)
-    query_pos = first_pos + jnp.arange(tok_rows, dtype=jnp.int32)
-    key_pos = first_pos - SPAN * tok_rows + jnp.arange((SPAN + 1) * tok_rows, dtype=jnp.int32)
-    same_doc = doc_index(doc_ends, query_pos)[:, None] == doc_index(doc_ends, key_pos)[None, :]
-    visible = same_doc & (key_pos[None, :] <= query_pos[:, None]) & (key_pos[None, :] >= 0)
-    packed = jnp.concatenate([key_heads, head_values], axis=1)
-    gone = [passed_along(packed, "ctx", distance) for distance in range(1, SPAN + 1)]
-    span_rows = jnp.concatenate(gone[::-1] + [packed], axis=0)
-    key_span_rows = span_rows[:, :key_value_width]
-    value_span_rows = span_rows[:, key_value_width:]
-    query_group = queries.reshape(tok_rows, query_group_size, HEAD_SIZE)
-    grad_group = output_gradient.reshape(tok_rows, query_group_size, HEAD_SIZE)
-    scores = (
-        jnp.einsum("tgd,kd->gtk", query_group, key_span_rows, preferred_element_type=jnp.float32)
-        * att_scale
-    )
-    scores = jnp.where(visible[None], scores, -jnp.inf)
-    row_max = jnp.max(scores, axis=-1, keepdims=True)
-    weights = jnp.exp(scores - row_max)
-    probs = weights / jnp.sum(weights, axis=-1, keepdims=True)
-    probs_low = probs.astype(jnp.bfloat16)
-    attended = jnp.einsum(
-        "gtk,kd->gtd", probs_low, value_span_rows, preferred_element_type=jnp.float32
-    )
-    delta = jnp.sum(jnp.transpose(grad_group, (1, 0, 2)).astype(jnp.float32) * attended, axis=-1)
-    dprobs = jnp.einsum(
-        "tgd,kd->gtk", grad_group, value_span_rows, preferred_element_type=jnp.float32
-    )
-    dscores = probs * (dprobs - delta[..., None])
-    dscores_low = dscores.astype(jnp.bfloat16)
-    query_grad = (
-        jnp.einsum("gtk,kd->tgd", dscores_low, key_span_rows, preferred_element_type=jnp.float32)
-        * att_scale
-    )
-    key_grad = (
-        jnp.einsum("gtk,tgd->kd", dscores_low, query_group, preferred_element_type=jnp.float32)
-        * att_scale
-    )
-    value_grad = jnp.einsum(
-        "gtk,tgd->kd", probs_low, grad_group, preferred_element_type=jnp.float32
-    )
-    query_low = query_grad.reshape(tok_rows, group_width).astype(jnp.bfloat16)
-    kv_grad = jnp.concatenate([key_grad, value_grad], axis=1)
-    far_terms = [
-        kv_grad[(SPAN - 1 - offset) * tok_rows : (SPAN - offset) * tok_rows]
-        for offset in range(SPAN)
-    ]
-    returned = kv_grad[SPAN * tok_rows :]
-    for distance in range(1, SPAN + 1):
-        returned = returned + passed_along(
-            far_terms[distance - 1].astype(jnp.bfloat16), "ctx", -distance
-        ).astype(jnp.float32)
-    kv_low = returned.astype(jnp.bfloat16)
-    joined = jnp.concatenate([query_low, kv_low], axis=1)
-    return weight_grads(activations, joined.T)
+    )(doc_lengths, activations, queries, key_heads, head_values, output_gradient)
 
 
 def solution(mesh):

time: 143 us -> 110 us (0.77)
  Pallas kernels: 65.7 us -> 100 us
  waiting for transfers between devices: 20.3 us -> 0 us
  other arithmetic: 18.9 us -> 0 us
  matrix products: 15.4 us -> 0 us
  starting transfers between devices: 13.9 us -> 0 us
    pallas_call x1, Pallas kernels: 65.7 us -> 100 us  [shards(): pl.pallas_call(kernel, out_shape=(jax.ShapeDtypeStruct((chunk, heads * HE...]
    ppermute x4 -> x0, waiting for transfers between devices: 20.3 us -> none  [passed_along(): lax.ppermute(value, axis, [(source, source + steps) for source in range(i...]
    dot_general x6 -> x0, matrix products: 15.4 us -> none  [the longest x1 3.09 us: shards(): jnp.einsum('tgd,kd->gtk', grad_group, value_span_rows, preferred_element_...]
    ppermute x4 -> x0, starting transfers between devices: 13.9 us -> none  [passed_along(): lax.ppermute(value, axis, [(source, source + steps) for source in range(i...]
    sub x1 -> x0, other arithmetic: 8.82 us -> none  [shards(): weights = jnp.exp(scores - row_max)]
    convert_element_type x2 -> x0, other arithmetic: 6.51 us -> none  [the longest x1 6.41 us: shards(): probs_low = probs.astype(jnp.bfloat16)]
    unnamed x17 -> x15, local copies, waits for them, and re-layouts: 5.1 us -> 8.61 us
    and x1 -> x0, other arithmetic: 1.5 us -> none  [shards(): same_doc & (key_pos[None, :] <= query_pos[:, None])]
  transfers between devices with their start and end apart: 4 -> 0, of which waited for: 3 -> 0; matrix products, arithmetic and copies ran while one was open for 6% -> 0% of each run, Pallas kernels for 0% -> 0%
where the time goes in v2:
time: 110 us; the launch traced here: 109 us
  Pallas kernels  100 us (91%)
  local copies, waits for them, and re-layouts  8.61 us (8%)
    pallas_call x1, Pallas kernels, shards(): pl.pallas_call(kernel, out_shape=(jax.ShapeDtypeStruct((chunk, heads * HE...  100 us
    unnamed x15, local copies, waits for them, and re-layouts  8.61 us

profile of v2, /device:TPU:32, one launch (start us, length us, event | category | flops | bytes accessed | tf_op | source)
XLA Modules:
  0.0 109.3 jit_solution(5887650835651131800)
XLA Ops:
  0.6 0.0 copy-start
  0.6 2.2 %copy-done = bf16[512,4096]{1,0:T(8,128)(2,1)S(1)} copy-done((bf16[512,4096]{1,0:T(8,128)(2,1)S(1)}, bf16[512,4096]{1,0:T(8,128)(2,1)}, u32[]{:S(2)}) %copy-start) | copy-done | bytes 4194328
  2.8 0.0 copy-start.1
  2.8 1.0 copy-done.1
  3.9 0.0 copy-start.2
  3.9 1.0 copy-done.2
  4.9 0.0 copy-start.3
  4.9 0.9 copy-done.3
  5.8 0.0 copy-start.4
  5.8 0.9 copy-done.4
  6.7 0.0 copy-start.5
  6.7 0.7 copy-done.5
  7.4 100.0 %shard_map.85 = (bf16[128,512]{1,0:T(8,128)(2,1)S(1)}, bf16[128,128]{1,0:T(8,128)(2,1)S(1)}, bf16[128,128]{1,0:T(8,128)(2,1)S(1)}) custom-call(s32[32]{0:T(128)S(1)} %copy-done.5, bf16[512,4096]{1,0:T(8,128)(2,1)S(1)} %copy-done, bf16[512,512]{1,0:T(8,128)(2,1)S(1)} %copy-done.1, bf16[512,128]{1,0:T(8,128)(2,1)S(1)} %copy-done.3, ...), custom_call_target="tpu_custom_call" | custom-call | tf_op jit(solution)/shard_map/pallas_call | solution.py:468
  107.4 0.7 copy.12
  108.1 0.6 copy.13
  108.7 0.6 copy.14
Async XLA Ops:
  0.6 2.2 %copy-start = (bf16[512,4096]{1,0:T(8,128)(2,1)S(1)}, bf16[512,4096]{1,0:T(8,128)(2,1)}, u32[]{:S(2)}) copy-start(bf16[512,4096]{1,0:T(8,128)(2,1)} %act.1) | copy-start | bytes 12582916
  2.8 1.0 copy-start.1
  3.9 1.0 copy-start.2
  4.9 0.9 copy-start.3
  5.8 0.9 copy-start.4
  6.7 0.7 copy-start.5

commit v3 on v2

v3 whole, which is shorter than its diff:
```python
import math

import jax
import jax.numpy as jnp
from jax import lax
from jax.experimental import pallas as pl
from jax.experimental.pallas import tpu as pltpu
from jax.sharding import PartitionSpec as P

HEAD_SIZE = 128
SPAN = 2
NX, NZ = 4, 8
NY, NCORE = 4, 2
WIDE = 256
REACH = 5
PARTS = ((0, 256), (256, 256), (512, 128), (640, 128))
MESH = pl.DeviceIdType.MESH


class Place:
    def __init__(self):
        self.c = lax.axis_index("ctx")
        self.t = lax.axis_index("tp")
        self.x = lax.div(self.c, NZ)
        self.z = lax.rem(self.c, NZ)
        self.y = lax.div(self.t, NCORE)
        self.core = lax.rem(self.t, NCORE)

    def at_x(self, step):
        return (lax.rem(self.x + step + NX, NX) * NZ + self.z, self.t)

    def at_z(self, step):
        return (self.x * NZ + lax.rem(self.z + step + NZ, NZ), self.t)

    def at_y(self, step):
        return (self.c, lax.rem(self.y + step + NY, NY) * NCORE + self.core)

    def at_c(self, step):
        count = NX * NZ
        return (lax.rem(self.c + step + count, count), self.t)

    def sibling(self):
        return (self.c, self.y * NCORE + 1 - self.core)

    def part(self, ystep, other_core):
        core = 1 - self.core if other_core else self.core
        return lax.rem(self.y + ystep + NY, NY) * NCORE + core


def remote(src, dst, send, recv, device):
    return pltpu.make_async_remote_copy(
        src_ref=src, dst_ref=dst, send_sem=send, recv_sem=recv, device_id=device, device_id_type=MESH
    )


class Acts:
    def __init__(self, place, act, abuf, local, sends, recvs):
        self.p, self.act, self.abuf, self.local, self.sends, self.recvs = place, act, abuf, local, sends, recvs
        self.tokens = act.shape[0]
        self.share = self.tokens // (NY * NCORE)
        self.quarter = act.shape[1] // NX

    def rows(self, part, begin=0, count=None):
        count = self.share if count is None else count
        return pl.ds(pl.multiple_of(part * self.share + begin, count), count)

    def own(self):
        cols = pl.ds(pl.multiple_of(self.p.x * self.quarter, self.quarter), self.quarter)
        return pltpu.make_async_copy(self.act.at[:, cols], self.abuf.at[0], self.local)

    def x_copy(self, step):
        there = lax.rem(self.p.x + step, NX)
        cols = pl.ds(pl.multiple_of(there * self.quarter, self.quarter), self.quarter)
        rows = self.rows(self.p.t)
        return remote(
            self.act.at[rows, cols],
            self.abuf.at[step, rows, :],
            self.sends.at[step - 1],
            self.recvs.at[step - 1],
            self.p.at_x(step),
        )

    def passed(self, rows, sem, device):
        piece = self.abuf.at[pl.ds(1, NX - 1), rows, :]
        return remote(piece, piece, self.sends.at[sem], self.recvs.at[sem], device)

    def y_copy(self, way, mine=True):
        step = 1 - 2 * way
        part = self.p.t if mine else self.p.part(-step, False)
        return self.passed(self.rows(part), 3 + way, self.p.at_y(step))

    def y_forward(self, way, mine=True):
        step = 1 - 2 * way
        half = self.share // 2
        rows = self.rows(self.p.part(-step if mine else 2, False), way * half, half)
        return self.passed(rows, 5 + way, self.p.at_y(step))

    def core_copy(self, which):
        return self.passed(self.rows(self.p.part((0, -1, 1, 2)[which], False)), 7 + which, self.p.sibling())

    def start(self):
        for step in (2, 1, 3):
            self.x_copy(step).start()
        self.own().start()

    def spread(self):
        for step in (1, 2, 3):
            self.x_copy(step).wait_recv()
        for way in range(2):
            self.y_copy(way).start()
        self.core_copy(0).start()

    def spread_on(self):
        for way in range(2):
            self.y_copy(way, False).wait_recv()
            self.y_forward(way).start()
        for way in range(2):
            self.core_copy(1 + way).start()

    def spread_last(self):
        for way in range(2):
            self.y_forward(way, False).wait_recv()
        self.core_copy(3).start()

    def landed(self):
        self.own().wait()
        for which in range(4):
            self.core_copy(which).wait_recv()

    def finish(self):
        for step in (1, 2, 3):
            self.x_copy(step).wait_send()
        for way in range(2):
            self.y_copy(way).wait_send()
            self.y_forward(way).wait_send()
        for which in range(4):
            self.core_copy(which).wait_send()


class Gather:
    def __init__(self, place, gbuf, sends, recvs):
        self.p, self.gbuf, self.sends, self.recvs = place, gbuf, sends, recvs
        self.tokens = gbuf.shape[1] // NX

    def copy(self, head, way):
        half = HEAD_SIZE // 2
        whole = pl.ds(pl.multiple_of(head * HEAD_SIZE, HEAD_SIZE), HEAD_SIZE)
        lower = pl.ds(pl.multiple_of(head * HEAD_SIZE, half), half)
        upper = pl.ds(pl.multiple_of(head * HEAD_SIZE + half, half), half)
        source, target, rows, step = ((0, 1, whole, 1), (0, 3, whole, -1), (1, 2, lower, 1), (3, 2, upper, -1))[way]
        return remote(
            self.gbuf.at[rows, pl.ds(source * self.tokens, self.tokens)],
            self.gbuf.at[rows, pl.ds(target * self.tokens, self.tokens)],
            self.sends.at[head, way],
            self.recvs.at[head, way],
            self.p.at_x(step),
        )

    def start(self, head):
        self.copy(head, 0).start()
        self.copy(head, 1).start()

    def forward(self, head):
        self.copy(head, 0).wait_recv()
        self.copy(head, 2).start()
        self.copy(head, 1).wait_recv()
        self.copy(head, 3).start()

    def landed(self, head):
        self.copy(head, 2).wait_recv()
        self.copy(head, 3).wait_recv()

    def finish(self, head):
        for way in range(4):
            self.copy(head, way).wait_send()


class Scatter:
    def __init__(self, place, terms, sbuf, rbuf, sends, recvs):
        self.p, self.terms, self.sbuf, self.rbuf, self.sends, self.recvs = place, terms, sbuf, rbuf, sends, recvs

    def rows(self, group, way, step):
        begin, count = PARTS[group]
        if step:
            return slice(begin, begin + count)
        return slice(begin + way * (count // 2), begin + (way + 1) * (count // 2))

    def copy(self, group, way, step):
        rows = self.rows(group, way, step)
        return remote(
            self.sbuf.at[way, step, rows, :],
            self.rbuf.at[way, step, rows, :],
            self.sends.at[group, way, step],
            self.recvs.at[group, way, step],
            self.p.at_z(1 - 2 * way),
        )

    def step(self, group, step):
        for way in range(2):
            owner = lax.rem(self.p.z + (1 - 2 * way) * (NZ // 2 - step) + NZ, NZ)
            if step:
                self.copy(group, way, step - 1).wait_recv()
            for half in range(2):
                if step == 0 and half != way:
                    continue
                rows = self.rows(group, half, 0)
                total = self.terms[owner, rows, :]
                if step > 1 or (step == 1 and half == way):
                    total += self.rbuf[way, step - 1, rows, :].astype(jnp.float32)
                self.sbuf[way, step, rows, :] = total.astype(jnp.bfloat16)
            self.copy(group, way, step).start()

    def result(self, group):
        last = NZ // 2 - 1
        rows = self.rows(group, 0, last)
        total = self.terms[self.p.z, rows, :]
        for way in range(2):
            self.copy(group, way, last).wait_recv()
            total += self.rbuf[way, last, rows, :].astype(jnp.float32)
        return total.T.astype(jnp.bfloat16)

    def finish(self, group):
        for way in range(2):
            for step in range(NZ // 2):
                self.copy(group, way, step).wait_send()


def weight_terms(group, abuf, gbuf, terms):
    begin, count = PARTS[group]
    rows = slice(begin, begin + count)
    width = terms.shape[2]
    per = WIDE // width

    def columns(n, carry):
        cols = pl.ds(pl.multiple_of(n * WIDE, WIDE), WIDE)
        acts = abuf[:, :, cols].reshape(gbuf.shape[1], WIDE)
        total = jnp.dot(gbuf[rows, :], acts, preferred_element_type=jnp.float32)
        for k in range(per):
            terms[n * per + k, rows, :] = total[:, k * width : (k + 1) * width]
        return carry

    lax.fori_loop(0, NZ // per, columns, 0)


class Span:
    def __init__(self, place, kbuf, vbuf, sends, recvs):
        self.p, self.bufs, self.sends, self.recvs = place, (kbuf, vbuf), sends, recvs

    def copy(self, which, hop):
        buf = self.bufs[which]
        source, target = (pl.ds(4, 2), pl.ds(2, 2)) if hop == 0 else (pl.ds(2, 2), pl.ds(0, 2))
        return remote(
            buf.at[source], buf.at[target], self.sends.at[which, hop], self.recvs.at[which, hop], self.p.at_c(1)
        )

    def finish(self):
        for which in range(2):
            for hop in range(2):
                self.copy(which, hop).wait_send()


class Return:
    def __init__(self, place, accs, sbuf, rbuf, sends, recvs):
        self.p, self.accs, self.sbuf, self.rbuf, self.sends, self.recvs = place, accs, sbuf, rbuf, sends, recvs

    def copy(self, which, hop):
        return remote(
            self.sbuf.at[which, hop],
            self.rbuf.at[which, hop],
            self.sends.at[which, hop],
            self.recvs.at[which, hop],
            self.p.at_c(-1),
        )

    def start(self, which, hop):
        if hop:
            self.copy(which, 0).wait_recv()
        for k in range(2):
            total = self.accs[which][2 * hop + k]
            if hop:
                total += self.rbuf[which, 0, k].astype(jnp.float32)
            self.sbuf[which, hop, k] = total.astype(jnp.bfloat16)
        self.copy(which, hop).start()

    def landed(self, which, factor, gbuf, row):
        self.copy(which, 1).wait_recv()
        for k in range(2):
            total = self.accs[which][4 + k] + self.rbuf[which, 1, k].astype(jnp.float32)
            gbuf[row : row + HEAD_SIZE, k * WIDE : (k + 1) * WIDE] = (total * factor).astype(jnp.bfloat16).T

    def finish(self):
        for which in range(2):
            for hop in range(2):
                self.copy(which, hop).wait_send()


def partners(place):
    others = [place.at_x(s) for s in (1, 2, 3)] + [place.at_y(s) for s in (1, -1)]
    return others + [place.sibling(), place.at_z(1), place.at_z(-1), place.at_c(1), place.at_c(-1)]


def doc_starts(docs, first, out):
    pos = first + lax.broadcasted_iota(jnp.int32, (1, out.shape[1]), 1)
    start = jnp.zeros_like(pos)
    end = jnp.int32(0)
    for n in range(docs.shape[0]):
        end = end + docs[n]
        start = jnp.where(pos >= end, end, start)
    out[...] = start


def near(qs):
    return slice(qs * WIDE, (qs + 1) * WIDE)


def reached(blocks):
    return [(qs, w, w - qs) for qs in range(2) for w in blocks if 0 <= w - qs < REACH]


def scores(h, blocks, base, starts, kbuf, qt, sc, top):
    row = lax.broadcasted_iota(jnp.int32, (WIDE, WIDE), 0)
    col = lax.broadcasted_iota(jnp.int32, (WIDE, WIDE), 1)
    tops = {}
    for qs, w, j in reached(blocks):
        s = jnp.dot(kbuf[w], qt[h, :, near(qs)], preferred_element_type=jnp.float32)
        seen = row >= starts[:, near(qs)] - (base + w * WIDE)
        if j == REACH - 1:
            seen &= row <= col
        s = jnp.where(seen, s, -jnp.inf)
        sc[h, qs, j] = s
        most = jnp.max(s, axis=0, keepdims=True)
        tops[qs] = jnp.maximum(tops[qs], most) if qs in tops else most
    for qs, most in tops.items():
        top[h, :, near(qs)] = jnp.maximum(top[h, :, near(qs)], most)


def value_products(h, blocks, vbuf, gt, dp):
    for qs, w, j in reached(blocks):
        dp[h, qs, j] = jnp.dot(vbuf[w], gt[h, :, near(qs)], preferred_element_type=jnp.float32)


def softmax(h, gh, sc, dp, top, inverse, mixed, dv):
    factor = HEAD_SIZE**-0.5 * math.log2(math.e)
    for qs in range(2):
        shift = top[h, :, near(qs)] * factor
        total = None
        for j in range(REACH):
            p = jnp.exp2(sc[h, qs, j] * factor - shift)
            sc[h, qs, j] = p
            part = jnp.sum(p, axis=0, keepdims=True)
            total = part if total is None else total + part
        inverse[h, :, near(qs)] = 1.0 / total
    for qs in range(2):
        scale = inverse[h, :, near(qs)]
        delta = None
        for j in range(REACH):
            p = sc[h, qs, j] * scale
            if qs + j >= 2:
                part = jnp.sum(p * dp[h, qs, j], axis=0, keepdims=True)
                delta = part if delta is None else delta + part
            dv[qs + j] += jnp.dot(p.astype(jnp.bfloat16), gh[h, near(qs)], preferred_element_type=jnp.float32)
        mixed[h, :, near(qs)] = delta


def score_grads(h, vbuf, kt, qh, gt, sc, dp, inverse, mixed, dk, gbuf):
    f32, bf16 = jnp.float32, jnp.bfloat16
    deltas = [mixed[h, :, near(qs)] for qs in range(2)]
    for qs, w, j in reached((0, 1)):
        d = jnp.dot(vbuf[w], gt[h, :, near(qs)], preferred_element_type=f32)
        dp[h, qs, j] = d
        deltas[qs] += jnp.sum(sc[h, qs, j] * inverse[h, :, near(qs)] * d, axis=0, keepdims=True)
    for qs in range(2):
        scale = inverse[h, :, near(qs)]
        dq = None
        for j in range(REACH):
            ds = (sc[h, qs, j] * scale * (dp[h, qs, j] - deltas[qs])).astype(bf16)
            dk[qs + j] += jnp.dot(ds, qh[h, near(qs)], preferred_element_type=f32)
            term = jnp.dot(kt[qs + j], ds, preferred_element_type=f32)
            dq = term if dq is None else dq + term
        rows = pl.ds(pl.multiple_of(h * HEAD_SIZE, HEAD_SIZE), HEAD_SIZE)
        gbuf[rows, near(qs)] = (dq * HEAD_SIZE**-0.5).astype(bf16)


def kernel(
    docs, act, q, k, v, g, wq, wk, wv,
    abuf, gbuf, terms, sbuf, rbuf, kbuf, vbuf, kt, qh, gh, qt, gt, sc, dp, dk, dv, starts, top, inverse, mixed,
    back_s, back_r, loads, local, as_, ar_, gs_, gr_, ss_, sr_, ks_, kr_, bs_, br_,
):
    place = Place()
    acts = Acts(place, act, abuf, local, as_, ar_)
    gather = Gather(place, gbuf, gs_, gr_)
    scatter = Scatter(place, terms, sbuf, rbuf, ss_, sr_)
    span = Span(place, kbuf, vbuf, ks_, kr_)
    back = Return(place, (dk, dv), back_s, back_r, bs_, br_)
    heads, tokens = qh.shape[0], qh.shape[1]
    first = place.c * tokens
    base = first - SPAN * tokens
    barrier = pltpu.get_barrier_semaphore()
    others = partners(place)
    for other in others:
        pl.semaphore_signal(barrier, inc=1, device_id=other, device_id_type=MESH)
    copies = [
        pltpu.make_async_copy(k, kbuf.at[pl.ds(4, 2)], loads.at[0]),
        pltpu.make_async_copy(v, vbuf.at[pl.ds(4, 2)], loads.at[1]),
    ]
    for h in range(heads):
        cols = pl.ds(h * HEAD_SIZE, HEAD_SIZE)
        copies.append(pltpu.make_async_copy(q.at[:, cols], qh.at[h], loads.at[2 + 2 * h]))
        copies.append(pltpu.make_async_copy(g.at[:, cols], gh.at[h], loads.at[3 + 2 * h]))
    for copy in copies:
        copy.start()
    doc_starts(docs, first, starts)
    dk[...] = jnp.zeros_like(dk)
    dv[...] = jnp.zeros_like(dv)
    top[...] = jnp.full_like(top, -jnp.inf)
    for copy in copies:
        copy.wait()
    pl.semaphore_wait(barrier, len(others))
    span.copy(0, 0).start()
    span.copy(1, 0).start()
    acts.start()

    def each_head(step):
        def body(h, carry):
            step(h)
            return carry

        lax.fori_loop(0, heads, body, 0)

    def turn(h):
        qt[h] = qh[h].T
        gt[h] = gh[h].T

    def own(h):
        scores(h, (4, 5), base, starts, kbuf, qt, sc, top)
        value_products(h, (4, 5), vbuf, gt, dp)

    def middle(h):
        scores(h, (2, 3), base, starts, kbuf, qt, sc, top)
        value_products(h, (2, 3), vbuf, gt, dp)

    def far(h):
        scores(h, (0, 1), base, starts, kbuf, qt, sc, top)
        softmax(h, gh, sc, dp, top, inverse, mixed, dv)

    def last(h):
        score_grads(h, vbuf, kt, qh, gt, sc, dp, inverse, mixed, dk, gbuf)
        gather.start(h)

        @pl.when(h == 2)
        def _():
            back.start(1, 1)
            acts.spread_on()

        @pl.when(h > 0)
        def _():
            gather.forward(h - 1)

    each_head(turn)
    span.copy(0, 0).wait_recv()
    span.copy(0, 1).start()
    each_head(own)
    span.copy(1, 0).wait_recv()
    span.copy(1, 1).start()
    each_head(middle)
    for n in (2, 3, 4, 5):
        kt[n] = kbuf[n].T
    span.copy(0, 1).wait_recv()
    for n in (0, 1):
        kt[n] = kbuf[n].T
    acts.spread()
    each_head(far)
    back.start(1, 0)
    span.copy(1, 1).wait_recv()
    each_head(last)
    back.start(0, 0)
    gather.forward(3)
    acts.spread_last()
    back.landed(1, 1.0, gbuf, 5 * HEAD_SIZE)
    gather.start(5)
    back.start(0, 1)
    acts.landed()
    gather.landed(0)
    gather.landed(1)
    weight_terms(0, abuf, gbuf, terms)
    scatter.step(0, 0)
    gather.forward(5)
    back.landed(0, HEAD_SIZE**-0.5, gbuf, 4 * HEAD_SIZE)
    gather.start(4)
    gather.landed(2)
    gather.landed(3)
    weight_terms(1, abuf, gbuf, terms)
    scatter.step(1, 0)
    scatter.step(0, 1)
    gather.landed(5)
    weight_terms(3, abuf, gbuf, terms)
    scatter.step(3, 0)
    gather.forward(4)
    scatter.step(0, 2)
    scatter.step(1, 1)
    scatter.step(3, 1)
    scatter.step(0, 3)
    scatter.step(1, 2)
    scatter.step(3, 2)
    gather.landed(4)
    weight_terms(2, abuf, gbuf, terms)
    scatter.step(2, 0)
    scatter.step(1, 3)
    scatter.step(3, 3)
    wq[:, 0:WIDE] = scatter.result(0)
    scatter.step(2, 1)
    wq[:, WIDE : 2 * WIDE] = scatter.result(1)
    scatter.step(2, 2)
    wv[...] = scatter.result(3)
    scatter.step(2, 3)
    wk[...] = scatter.result(2)
    acts.finish()
    span.finish()
    back.finish()
    for n in range(heads + 2):
        gather.finish(n)
    for group in range(len(PARTS)):
        scatter.finish(group)


def shards(doc_lengths, activations, queries, key_heads, head_values, output_gradient):
    tokens, features = activations.shape
    heads = queries.shape[1] // HEAD_SIZE
    quarter = features // NX
    chunk = quarter // NZ
    blocks = (SPAN + 1) * tokens // WIDE
    width = (heads + 2) * HEAD_SIZE
    bf16, f32 = jnp.bfloat16, jnp.float32
    dma = pltpu.SemaphoreType.DMA
    vmem = pl.BlockSpec(memory_space=pltpu.VMEM)
    return pl.pallas_call(
        kernel,
        out_shape=(
            jax.ShapeDtypeStruct((chunk, heads * HEAD_SIZE), bf16),
            jax.ShapeDtypeStruct((chunk, HEAD_SIZE), bf16),
            jax.ShapeDtypeStruct((chunk, HEAD_SIZE), bf16),
        ),
        in_specs=[pl.BlockSpec(memory_space=pltpu.SMEM)] + [pl.BlockSpec(memory_space=pl.ANY)] * 5,
        out_specs=[vmem] * 3,
        scratch_shapes=[
            pltpu.VMEM((NX, tokens, quarter), bf16),
            pltpu.VMEM((width, NX * tokens), bf16),
            pltpu.VMEM((NZ, width, chunk), f32),
            pltpu.VMEM((2, NZ // 2, width, chunk), bf16),
            pltpu.VMEM((2, NZ // 2, width, chunk), bf16),
            pltpu.VMEM((blocks, WIDE, HEAD_SIZE), bf16),
            pltpu.VMEM((blocks, WIDE, HEAD_SIZE), bf16),
            pltpu.VMEM((blocks, HEAD_SIZE, WIDE), bf16),
            pltpu.VMEM((heads, tokens, HEAD_SIZE), bf16),
            pltpu.VMEM((heads, tokens, HEAD_SIZE), bf16),
            pltpu.VMEM((heads, HEAD_SIZE, tokens), bf16),
            pltpu.VMEM((heads, HEAD_SIZE, tokens), bf16),
            pltpu.VMEM((heads, 2, REACH, WIDE, WIDE), f32),
            pltpu.VMEM((heads, 2, REACH, WIDE, WIDE), f32),
            pltpu.VMEM((blocks, WIDE, HEAD_SIZE), f32),
            pltpu.VMEM((blocks, WIDE, HEAD_SIZE), f32),
            pltpu.VMEM((1, tokens), jnp.int32),
            pltpu.VMEM((heads, 1, tokens), f32),
            pltpu.VMEM((heads, 1, tokens), f32),
            pltpu.VMEM((heads, 1, tokens), f32),
            pltpu.VMEM((2, 2, 2, WIDE, HEAD_SIZE), bf16),
            pltpu.VMEM((2, 2, 2, WIDE, HEAD_SIZE), bf16),
            dma((2 + 2 * heads,)),
            dma,
            dma((11,)),
            dma((11,)),
            dma((heads + 2, 4)),
            dma((heads + 2, 4)),
            dma((len(PARTS), 2, NZ // 2)),
            dma((len(PARTS), 2, NZ // 2)),
            dma((2, 2)),
            dma((2, 2)),
            dma((2, 2)),
            dma((2, 2)),
        ],
        compiler_params=pltpu.CompilerParams(
            collective_id=0, has_side_effects=True, vmem_limit_bytes=56 * 2**20
        ),
    )(
        doc_lengths,
        activations,
        queries,
        key_heads.reshape(-1, WIDE, HEAD_SIZE),
        head_values.reshape(-1, WIDE, HEAD_SIZE),
        output_gradient,
    )


def solution(mesh):
    return jax.shard_map(
        shards,
        mesh=mesh,
        in_specs=(
            P(),
            P("ctx", None),
            P("ctx", "tp"),
            P("ctx", "tp"),
            P("ctx", "tp"),
            P("ctx", "tp"),
        ),
        out_specs=(P("ctx", "tp"), P("ctx", "tp"), P("ctx", "tp")),
        check_vma=False,
    )
```

time: 110 us -> 91.2 us (0.83); the launches traced: 109 us -> 89.4 us
  Pallas kernels: 100 us -> 84.4 us
  local copies, waits for them, and re-layouts: 8.61 us -> 4.32 us
    pallas_call x1, Pallas kernels: 100 us -> 84.4 us  [shards(): pl.pallas_call(kernel, out_shape=(jax.ShapeDtypeStruct((chunk, heads * HE...]
    unnamed x15 -> x3, local copies, waits for them, and re-layouts: 8.61 us -> 4.32 us
where the time goes in v3:
time: 91.2 us; the launch traced here: 89.4 us
  Pallas kernels  84.4 us (93%)
  local copies, waits for them, and re-layouts  4.32 us (5%)
    pallas_call x1, Pallas kernels, shards(): pl.pallas_call(kernel, out_shape=(jax.ShapeDtypeStruct((chunk, heads * HE...  84.4 us
    unnamed x3, local copies, waits for them, and re-layouts  4.32 us

profile of v3, /device:TPU:32, one launch (start us, length us, event | category | flops | bytes accessed | tf_op | source)
XLA Modules:
  0.0 89.4 jit_solution(13562550840004228731)
XLA Ops:
  0.6 84.4 %shard_map.85 = (bf16[128,512]{1,0:T(8,128)(2,1)}, bf16[128,128]{1,0:T(8,128)(2,1)}, bf16[128,128]{1,0:T(8,128)(2,1)}) custom-call(s32[32]{0:T(128)} %docs.1, bf16[512,4096]{1,0:T(8,128)(2,1)} %act.1, bf16[512,512]{1,0:T(8,128)(2,1)} %q.1, bf16[2,256,128]{2,1,0:T(8,128)(2,1)} %bitcast.2, bf16[2,256,128]{2,1,0:T(8,128)(2,1)} %bitcast.3, bf16[512,512]{1,0:T(8,128)(2,1)} %g.1), custom_call_target="tpu_custom_call" | custom-call | tf_op jit(solution)/shard_map/pallas_call | solution.py:536
  85.0 1.6 %copy.12 = bf16[128,512]{1,0:T(8,128)(2,1)} copy(bf16[128,512]{1,0:T(8,128)(2,1)} %get-tuple-element.6) | data formatting | bytes 262144
  86.6 1.4 %copy.13 = bf16[128,128]{1,0:T(8,128)(2,1)} copy(bf16[128,128]{1,0:T(8,128)(2,1)} %get-tuple-element.7) | data formatting | bytes 65536
  88.0 1.4 %copy.14 = bf16[128,128]{1,0:T(8,128)(2,1)} copy(bf16[128,128]{1,0:T(8,128)(2,1)} %get-tuple-element.8) | data formatting | bytes 65536

commit v4 on v3

--- a/solution.py
+++ b/solution.py
@@ -13,6 +13,7 @@
 NY, NCORE = 4, 2
 WIDE = 256
 REACH = 5
+AHEAD = 96
 PARTS = ((0, 256), (256, 256), (512, 128), (640, 128))
 MESH = pl.DeviceIdType.MESH
 
@@ -54,7 +55,8 @@
 
 
 class Acts:
-    def __init__(self, place, act, abuf, local, sends, recvs):
+    def __init__(self, place, act, abuf, relay, local, sends, recvs):
+        self.relay = relay
         self.p, self.act, self.abuf, self.local, self.sends, self.recvs = place, act, abuf, local, sends, recvs
         self.tokens = act.shape[0]
         self.share = self.tokens // (NY * NCORE)
@@ -68,17 +70,27 @@
         cols = pl.ds(pl.multiple_of(self.p.x * self.quarter, self.quarter), self.quarter)
         return pltpu.make_async_copy(self.act.at[:, cols], self.abuf.at[0], self.local)
 
-    def x_copy(self, step):
-        there = lax.rem(self.p.x + step, NX)
-        cols = pl.ds(pl.multiple_of(there * self.quarter, self.quarter), self.quarter)
+    def quarter_of(self, step):
+        there = lax.rem(self.p.x + step + NX, NX)
+        return pl.ds(pl.multiple_of(there * self.quarter, self.quarter), self.quarter)
+
+    def x_copy(self, way):
+        step = 1 - 2 * way
         rows = self.rows(self.p.t)
-        return remote(
-            self.act.at[rows, cols],
-            self.abuf.at[step, rows, :],
-            self.sends.at[step - 1],
-            self.recvs.at[step - 1],
-            self.p.at_x(step),
-        )
+        source, target = self.act.at[rows, self.quarter_of(step)], self.abuf.at[step % NX, rows, :]
+        return remote(source, target, self.sends.at[way], self.recvs.at[way], self.p.at_x(step))
+
+    def x_relay(self, way):
+        half = self.share // 2
+        source = self.act.at[self.rows(self.p.t, way * half, half), self.quarter_of(2)]
+        device = self.p.at_x(1 - 2 * way)
+        return remote(source, self.relay.at[way], self.sends.at[11 + way], self.recvs.at[11 + way], device)
+
+    def x_forward(self, way):
+        half = self.share // 2
+        target = self.abuf.at[2, self.rows(self.p.t, way * half, half), :]
+        device = self.p.at_x(1 - 2 * way)
+        return remote(self.relay.at[way], target, self.sends.at[13 + way], self.recvs.at[13 + way], device)
 
     def passed(self, rows, sem, device):
         piece = self.abuf.at[pl.ds(1, NX - 1), rows, :]
@@ -99,13 +111,20 @@
         return self.passed(self.rows(self.p.part((0, -1, 1, 2)[which], False)), 7 + which, self.p.sibling())
 
     def start(self):
-        for step in (2, 1, 3):
-            self.x_copy(step).start()
-        self.own().start()
+        for way in range(2):
+            self.x_relay(way).start()
+        for way in range(2):
+            self.x_copy(way).start()
+
+    def forward(self):
+        for way in range(2):
+            self.x_relay(way).wait_recv()
+            self.x_forward(way).start()
 
     def spread(self):
-        for step in (1, 2, 3):
-            self.x_copy(step).wait_recv()
+        for way in range(2):
+            self.x_copy(way).wait_recv()
+            self.x_forward(way).wait_recv()
         for way in range(2):
             self.y_copy(way).start()
         self.core_copy(0).start()
@@ -128,9 +147,10 @@
             self.core_copy(which).wait_recv()
 
     def finish(self):
-        for step in (1, 2, 3):
-            self.x_copy(step).wait_send()
-        for way in range(2):
+        for way in range(2):
+            self.x_copy(way).wait_send()
+            self.x_relay(way).wait_send()
+            self.x_forward(way).wait_send()
             self.y_copy(way).wait_send()
             self.y_forward(way).wait_send()
         for which in range(4):
@@ -143,10 +163,10 @@
         self.tokens = gbuf.shape[1] // NX
 
     def copy(self, head, way):
-        half = HEAD_SIZE // 2
+        rest = HEAD_SIZE - AHEAD
         whole = pl.ds(pl.multiple_of(head * HEAD_SIZE, HEAD_SIZE), HEAD_SIZE)
-        lower = pl.ds(pl.multiple_of(head * HEAD_SIZE, half), half)
-        upper = pl.ds(pl.multiple_of(head * HEAD_SIZE + half, half), half)
+        lower = pl.ds(pl.multiple_of(head * HEAD_SIZE, HEAD_SIZE), AHEAD)
+        upper = pl.ds(pl.multiple_of(head * HEAD_SIZE + AHEAD, rest), rest)
         source, target, rows, step = ((0, 1, whole, 1), (0, 3, whole, -1), (1, 2, lower, 1), (3, 2, upper, -1))[way]
         return remote(
             self.gbuf.at[rows, pl.ds(source * self.tokens, self.tokens)],
@@ -217,12 +237,40 @@
         for way in range(2):
             self.copy(group, way, last).wait_recv()
             total += self.rbuf[way, last, rows, :].astype(jnp.float32)
-        return total.T.astype(jnp.bfloat16)
+        return total.astype(jnp.bfloat16)
 
     def finish(self, group):
         for way in range(2):
             for step in range(NZ // 2):
                 self.copy(group, way, step).wait_send()
+
+
+class Direct:
+    def __init__(self, place, group, terms, sbuf, rbuf, sends, recvs):
+        self.p, self.terms, self.sbuf, self.rbuf, self.sends, self.recvs = place, terms, sbuf, rbuf, sends, recvs
+        begin, count = PARTS[group]
+        self.rows = slice(begin, begin + count)
+
+    def copy(self, step):
+        n = step - 1
+        return remote(self.sbuf.at[n], self.rbuf.at[n], self.sends.at[n], self.recvs.at[n], self.p.at_z(step))
+
+    def start(self):
+        for step in (4, 3, 5, 2, 6, 1, 7):
+            owner = lax.rem(self.p.z + step, NZ)
+            self.sbuf[step - 1] = self.terms[owner, self.rows, :].astype(jnp.bfloat16)
+            self.copy(step).start()
+
+    def result(self):
+        total = self.terms[self.p.z, self.rows, :]
+        for step in (1, 7, 2, 6, 3, 5, 4):
+            self.copy(step).wait_recv()
+            total += self.rbuf[step - 1].astype(jnp.float32)
+        return total.astype(jnp.bfloat16)
+
+    def finish(self):
+        for step in range(1, NZ):
+            self.copy(step).wait_send()
 
 
 def weight_terms(group, abuf, gbuf, terms):
@@ -295,8 +343,8 @@
 
 
 def partners(place):
-    others = [place.at_x(s) for s in (1, 2, 3)] + [place.at_y(s) for s in (1, -1)]
-    return others + [place.sibling(), place.at_z(1), place.at_z(-1), place.at_c(1), place.at_c(-1)]
+    others = [place.at_x(s) for s in (1, -1)] + [place.at_y(s) for s in (1, -1)]
+    return others + [place.sibling(), place.at_c(1), place.at_c(-1)] + [place.at_z(s) for s in range(1, NZ)]
 
 
 def doc_starts(docs, first, out):
@@ -382,16 +430,17 @@
 
 
 def kernel(
-    docs, act, q, k, v, g, wq, wk, wv,
-    abuf, gbuf, terms, sbuf, rbuf, kbuf, vbuf, kt, qh, gh, qt, gt, sc, dp, dk, dv, starts, top, inverse, mixed,
-    back_s, back_r, loads, local, as_, ar_, gs_, gr_, ss_, sr_, ks_, kr_, bs_, br_,
+    docs, act, q, k, v, g, out,
+    abuf, relay, gbuf, terms, sbuf, rbuf, kbuf, vbuf, kt, qh, gh, qt, gt, sc, dp, dk, dv, starts, top, inverse, mixed,
+    back_s, back_r, dir_s, dir_r, loads, local, as_, ar_, gs_, gr_, ss_, sr_, ks_, kr_, bs_, br_, ds_, dr_,
 ):
     place = Place()
-    acts = Acts(place, act, abuf, local, as_, ar_)
+    acts = Acts(place, act, abuf, relay, local, as_, ar_)
     gather = Gather(place, gbuf, gs_, gr_)
     scatter = Scatter(place, terms, sbuf, rbuf, ss_, sr_)
     span = Span(place, kbuf, vbuf, ks_, kr_)
     back = Return(place, (dk, dv), back_s, back_r, bs_, br_)
+    direct = Direct(place, 2, terms, dir_s, dir_r, ds_, dr_)
     heads, tokens = qh.shape[0], qh.shape[1]
     first = place.c * tokens
     base = first - SPAN * tokens
@@ -409,16 +458,18 @@
         copies.append(pltpu.make_async_copy(g.at[:, cols], gh.at[h], loads.at[3 + 2 * h]))
     for copy in copies:
         copy.start()
+    for copy in copies[:2]:
+        copy.wait()
+    pl.semaphore_wait(barrier, len(others))
+    span.copy(0, 0).start()
+    span.copy(1, 0).start()
+    acts.own().start()
     doc_starts(docs, first, starts)
     dk[...] = jnp.zeros_like(dk)
     dv[...] = jnp.zeros_like(dv)
     top[...] = jnp.full_like(top, -jnp.inf)
-    for copy in copies:
+    for copy in copies[2:]:
         copy.wait()
-    pl.semaphore_wait(barrier, len(others))
-    span.copy(0, 0).start()
-    span.copy(1, 0).start()
-    acts.start()
 
     def each_head(step):
         def body(h, carry):
@@ -447,14 +498,13 @@
         score_grads(h, vbuf, kt, qh, gt, sc, dp, inverse, mixed, dk, gbuf)
         gather.start(h)
 
+        @pl.when(h == 1)
+        def _():
+            back.start(1, 1)
+
         @pl.when(h == 2)
         def _():
-            back.start(1, 1)
-            acts.spread_on()
-
-        @pl.when(h > 0)
-        def _():
-            gather.forward(h - 1)
+            acts.spread()
 
     each_head(turn)
     span.copy(0, 0).wait_recv()
@@ -462,65 +512,77 @@
     each_head(own)
     span.copy(1, 0).wait_recv()
     span.copy(1, 1).start()
+    acts.start()
     each_head(middle)
     for n in (2, 3, 4, 5):
         kt[n] = kbuf[n].T
     span.copy(0, 1).wait_recv()
     for n in (0, 1):
         kt[n] = kbuf[n].T
-    acts.spread()
     each_head(far)
     back.start(1, 0)
+    acts.forward()
     span.copy(1, 1).wait_recv()
     each_head(last)
     back.start(0, 0)
-    gather.forward(3)
-    acts.spread_last()
+    gather.forward(0)
     back.landed(1, 1.0, gbuf, 5 * HEAD_SIZE)
     gather.start(5)
+    gather.forward(1)
     back.start(0, 1)
-    acts.landed()
+    gather.forward(2)
+    acts.spread_on()
+    gather.forward(3)
+    back.landed(0, HEAD_SIZE**-0.5, gbuf, 4 * HEAD_SIZE)
+    gather.start(4)
+    acts.spread_last()
+    gather.forward(5)
     gather.landed(0)
     gather.landed(1)
+    acts.landed()
     weight_terms(0, abuf, gbuf, terms)
     scatter.step(0, 0)
-    gather.forward(5)
-    back.landed(0, HEAD_SIZE**-0.5, gbuf, 4 * HEAD_SIZE)
-    gather.start(4)
     gather.landed(2)
     gather.landed(3)
     weight_terms(1, abuf, gbuf, terms)
     scatter.step(1, 0)
+    gather.forward(4)
     scatter.step(0, 1)
     gather.landed(5)
     weight_terms(3, abuf, gbuf, terms)
     scatter.step(3, 0)
-    gather.forward(4)
+    scatter.step(1, 1)
     scatter.step(0, 2)
-    scatter.step(1, 1)
-    scatter.step(3, 1)
-    scatter.step(0, 3)
-    scatter.step(1, 2)
-    scatter.step(3, 2)
     gather.landed(4)
     weight_terms(2, abuf, gbuf, terms)
-    scatter.step(2, 0)
+    direct.start()
+    scatter.step(3, 1)
+    scatter.step(1, 2)
+    scatter.step(0, 3)
+    scatter.step(3, 2)
     scatter.step(1, 3)
+    out[0:WIDE, :] = scatter.result(0)
     scatter.step(3, 3)
-    wq[:, 0:WIDE] = scatter.result(0)
-    scatter.step(2, 1)
-    wq[:, WIDE : 2 * WIDE] = scatter.result(1)
-    scatter.step(2, 2)
-    wv[...] = scatter.result(3)
-    scatter.step(2, 3)
-    wk[...] = scatter.result(2)
+    out[WIDE : 2 * WIDE, :] = scatter.result(1)
+    out[4 * HEAD_SIZE : 5 * HEAD_SIZE, :] = direct.result()
+    out[5 * HEAD_SIZE : 6 * HEAD_SIZE, :] = scatter.result(3)
     acts.finish()
     span.finish()
     back.finish()
+    direct.finish()
     for n in range(heads + 2):
         gather.finish(n)
-    for group in range(len(PARTS)):
+    for group in (0, 1, 3):
         scatter.finish(group)
+
+
+def turned(total, wq, wk, wv):
+    columns = wq.shape[1]
+    for n in range(columns // HEAD_SIZE):
+        rows = slice(n * HEAD_SIZE, (n + 1) * HEAD_SIZE)
+        wq[:, rows] = total[rows, :].T
+    wk[...] = total[columns : columns + HEAD_SIZE, :].T
+    wv[...] = total[columns + HEAD_SIZE : columns + 2 * HEAD_SIZE, :].T
 
 
 def shards(doc_lengths, activations, queries, key_heads, head_values, output_gradient):
@@ -533,17 +595,14 @@
     bf16, f32 = jnp.bfloat16, jnp.float32
     dma = pltpu.SemaphoreType.DMA
     vmem = pl.BlockSpec(memory_space=pltpu.VMEM)
-    return pl.pallas_call(
+    total = pl.pallas_call(
         kernel,
-        out_shape=(
-            jax.ShapeDtypeStruct((chunk, heads * HEAD_SIZE), bf16),
-            jax.ShapeDtypeStruct((chunk, HEAD_SIZE), bf16),
-            jax.ShapeDtypeStruct((chunk, HEAD_SIZE), bf16),
-        ),
+        out_shape=jax.ShapeDtypeStruct((width, chunk), bf16),
         in_specs=[pl.BlockSpec(memory_space=pltpu.SMEM)] + [pl.BlockSpec(memory_space=pl.ANY)] * 5,
-        out_specs=[vmem] * 3,
+        out_specs=vmem,
         scratch_shapes=[
             pltpu.VMEM((NX, tokens, quarter), bf16),
+            pltpu.VMEM((2, tokens // (2 * NY * NCORE), quarter), bf16),
             pltpu.VMEM((width, NX * tokens), bf16),
             pltpu.VMEM((NZ, width, chunk), f32),
             pltpu.VMEM((2, NZ // 2, width, chunk), bf16),
@@ -565,10 +624,12 @@
             pltpu.VMEM((heads, 1, tokens), f32),
             pltpu.VMEM((2, 2, 2, WIDE, HEAD_SIZE), bf16),
             pltpu.VMEM((2, 2, 2, WIDE, HEAD_SIZE), bf16),
+            pltpu.VMEM((NZ - 1, HEAD_SIZE, chunk), bf16),
+            pltpu.VMEM((NZ - 1, HEAD_SIZE, chunk), bf16),
             dma((2 + 2 * heads,)),
             dma,
-            dma((11,)),
-            dma((11,)),
+            dma((15,)),
+            dma((15,)),
             dma((heads + 2, 4)),
             dma((heads + 2, 4)),
             dma((len(PARTS), 2, NZ // 2)),
@@ -577,6 +638,8 @@
             dma((2, 2)),
             dma((2, 2)),
             dma((2, 2)),
+            dma((NZ - 1,)),
+            dma((NZ - 1,)),
         ],
         compiler_params=pltpu.CompilerParams(
             collective_id=0, has_side_effects=True, vmem_limit_bytes=56 * 2**20
@@ -589,6 +652,16 @@
         head_values.reshape(-1, WIDE, HEAD_SIZE),
         output_gradient,
     )
+    return pl.pallas_call(
+        turned,
+        out_shape=(
+            jax.ShapeDtypeStruct((chunk, heads * HEAD_SIZE), bf16),
+            jax.ShapeDtypeStruct((chunk, HEAD_SIZE), bf16),
+            jax.ShapeDtypeStruct((chunk, HEAD_SIZE), bf16),
+        ),
+        in_specs=[vmem],
+        out_specs=[vmem] * 3,
+    )(total)
 
 
 def solution(mesh):

time: 91.2 us -> 84.9 us (0.931)
  local copies, waits for them, and re-layouts: 4.32 us -> 0 us
  Pallas kernels: 84.4 us -> 83 us
    unnamed x3 -> x0, local copies, waits for them, and re-layouts: 4.32 us -> none
    pallas_call x1 -> x2, Pallas kernels: 84.4 us -> 83 us  [the longest x1 81.3 us: shards(): pl.pallas_call(kernel, out_shape=jax.ShapeDtypeStruct((width, chunk), bf1...]
where the time goes in v4:
time: 84.9 us; the launch traced here: 83.6 us
  Pallas kernels  83 us (98%)
    pallas_call x1, Pallas kernels, shards(): pl.pallas_call(kernel, out_shape=jax.ShapeDtypeStruct((width, chunk), bf1...  81.3 us
    pallas_call x1, Pallas kernels, shards(): pl.pallas_call(turned, out_shape=(jax.ShapeDtypeStruct((chunk, heads * HE...  1.7 us

profile of v4, /device:TPU:32, one launch (start us, length us, event | category | flops | bytes accessed | tf_op | source)
XLA Modules:
  0.0 83.6 jit_solution(720980334840244024)
XLA Ops:
  0.6 81.3 %shard_map.85.total = bf16[768,128]{1,0:T(8,128)(2,1)} custom-call(s32[32]{0:T(128)} %docs.1, bf16[512,4096]{1,0:T(8,128)(2,1)} %act.1, bf16[512,512]{1,0:T(8,128)(2,1)} %q.1, bf16[2,256,128]{2,1,0:T(8,128)(2,1)} %bitcast.2, bf16[2,256,128]{2,1,0:T(8,128)(2,1)} %bitcast.3, bf16[512,512]{1,0:T(8,128)(2,1)} %g.1), custom_call_target="tpu_custom_call" | custom-call | tf_op jit(solution)/shard_map/pallas_call | solution.py:598
  81.9 1.7 %shard_map.86 = (bf16[128,512]{1,0:T(8,128)(2,1)}, bf16[128,128]{1,0:T(8,128)(2,1)}, bf16[128,128]{1,0:T(8,128)(2,1)}) custom-call(bf16[768,128]{1,0:T(8,128)(2,1)} %shard_map.85.total), custom_call_target="tpu_custom_call" | custom-call | tf_op jit(solution)/shard_map/pallas_call | solution.py:655

commit v5 on v4

--- a/solution.py
+++ b/solution.py
@@ -14,7 +14,7 @@
 WIDE = 256
 REACH = 5
 AHEAD = 96
-PARTS = ((0, 256), (256, 256), (512, 128), (640, 128))
+PARTS = ((0, 256), (256, 256), (512, 256))
 MESH = pl.DeviceIdType.MESH
 
 
@@ -84,31 +84,32 @@
         half = self.share // 2
         source = self.act.at[self.rows(self.p.t, way * half, half), self.quarter_of(2)]
         device = self.p.at_x(1 - 2 * way)
-        return remote(source, self.relay.at[way], self.sends.at[11 + way], self.recvs.at[11 + way], device)
+        return remote(source, self.relay.at[way], self.sends.at[2 + way], self.recvs.at[2 + way], device)
 
     def x_forward(self, way):
         half = self.share // 2
         target = self.abuf.at[2, self.rows(self.p.t, way * half, half), :]
         device = self.p.at_x(1 - 2 * way)
-        return remote(self.relay.at[way], target, self.sends.at[13 + way], self.recvs.at[13 + way], device)
-
-    def passed(self, rows, sem, device):
-        piece = self.abuf.at[pl.ds(1, NX - 1), rows, :]
+        return remote(self.relay.at[way], target, self.sends.at[4 + way], self.recvs.at[4 + way], device)
+
+    def passed(self, slot, rows, sem, device):
+        piece = self.abuf.at[slot, rows, :]
         return remote(piece, piece, self.sends.at[sem], self.recvs.at[sem], device)
 
-    def y_copy(self, way, mine=True):
+    def y_copy(self, slot, way, mine=True):
         step = 1 - 2 * way
         part = self.p.t if mine else self.p.part(-step, False)
-        return self.passed(self.rows(part), 3 + way, self.p.at_y(step))
-
-    def y_forward(self, way, mine=True):
+        return self.passed(slot, self.rows(part), 8 * slot + way, self.p.at_y(step))
+
+    def y_forward(self, slot, way, mine=True):
         step = 1 - 2 * way
         half = self.share // 2
         rows = self.rows(self.p.part(-step if mine else 2, False), way * half, half)
-        return self.passed(rows, 5 + way, self.p.at_y(step))
-
-    def core_copy(self, which):
-        return self.passed(self.rows(self.p.part((0, -1, 1, 2)[which], False)), 7 + which, self.p.sibling())
+        return self.passed(slot, rows, 8 * slot + 2 + way, self.p.at_y(step))
+
+    def core_copy(self, slot, which):
+        rows = self.rows(self.p.part((0, -1, 1, 2)[which], False))
+        return self.passed(slot, rows, 8 * slot + 4 + which, self.p.sibling())
 
     def start(self):
         for way in range(2):
@@ -121,40 +122,45 @@
             self.x_relay(way).wait_recv()
             self.x_forward(way).start()
 
-    def spread(self):
-        for way in range(2):
-            self.x_copy(way).wait_recv()
-            self.x_forward(way).wait_recv()
-        for way in range(2):
-            self.y_copy(way).start()
-        self.core_copy(0).start()
-
-    def spread_on(self):
-        for way in range(2):
-            self.y_copy(way, False).wait_recv()
-            self.y_forward(way).start()
-        for way in range(2):
-            self.core_copy(1 + way).start()
-
-    def spread_last(self):
-        for way in range(2):
-            self.y_forward(way, False).wait_recv()
-        self.core_copy(3).start()
+    def spread(self, slot):
+        if slot == 2:
+            for way in range(2):
+                self.x_forward(way).wait_recv()
+        else:
+            self.x_copy(slot // 2).wait_recv()
+        for way in range(2):
+            self.y_copy(slot, way).start()
+        self.core_copy(slot, 0).start()
+
+    def spread_on(self, slot):
+        for way in range(2):
+            self.y_copy(slot, way, False).wait_recv()
+            self.y_forward(slot, way).start()
+        for way in range(2):
+            self.core_copy(slot, 1 + way).start()
+
+    def spread_last(self, slot):
+        for way in range(2):
+            self.y_forward(slot, way, False).wait_recv()
+        self.core_copy(slot, 3).start()
 
     def landed(self):
         self.own().wait()
-        for which in range(4):
-            self.core_copy(which).wait_recv()
+        for slot in range(1, NX):
+            for which in range(4):
+                self.core_copy(slot, which).wait_recv()
 
     def finish(self):
         for way in range(2):
             self.x_copy(way).wait_send()
             self.x_relay(way).wait_send()
             self.x_forward(way).wait_send()
-            self.y_copy(way).wait_send()
-            self.y_forward(way).wait_send()
-        for which in range(4):
-            self.core_copy(which).wait_send()
+        for slot in range(1, NX):
+            for way in range(2):
+                self.y_copy(slot, way).wait_send()
+                self.y_forward(slot, way).wait_send()
+            for which in range(4):
+                self.core_copy(slot, which).wait_send()
 
 
 class Gather:
@@ -245,34 +251,6 @@
                 self.copy(group, way, step).wait_send()
 
 
-class Direct:
-    def __init__(self, place, group, terms, sbuf, rbuf, sends, recvs):
-        self.p, self.terms, self.sbuf, self.rbuf, self.sends, self.recvs = place, terms, sbuf, rbuf, sends, recvs
-        begin, count = PARTS[group]
-        self.rows = slice(begin, begin + count)
-
-    def copy(self, step):
-        n = step - 1
-        return remote(self.sbuf.at[n], self.rbuf.at[n], self.sends.at[n], self.recvs.at[n], self.p.at_z(step))
-
-    def start(self):
-        for step in (4, 3, 5, 2, 6, 1, 7):
-            owner = lax.rem(self.p.z + step, NZ)
-            self.sbuf[step - 1] = self.terms[owner, self.rows, :].astype(jnp.bfloat16)
-            self.copy(step).start()
-
-    def result(self):
-        total = self.terms[self.p.z, self.rows, :]
-        for step in (1, 7, 2, 6, 3, 5, 4):
-            self.copy(step).wait_recv()
-            total += self.rbuf[step - 1].astype(jnp.float32)
-        return total.astype(jnp.bfloat16)
-
-    def finish(self):
-        for step in range(1, NZ):
-            self.copy(step).wait_send()
-
-
 def weight_terms(group, abuf, gbuf, terms):
     begin, count = PARTS[group]
     rows = slice(begin, begin + count)
@@ -344,7 +322,7 @@
 
 def partners(place):
     others = [place.at_x(s) for s in (1, -1)] + [place.at_y(s) for s in (1, -1)]
-    return others + [place.sibling(), place.at_c(1), place.at_c(-1)] + [place.at_z(s) for s in range(1, NZ)]
+    return others + [place.sibling(), place.at_c(1), place.at_c(-1)] + [place.at_z(1), place.at_z(-1)]
 
 
 def doc_starts(docs, first, out):
@@ -432,7 +410,7 @@
 def kernel(
     docs, act, q, k, v, g, out,
     abuf, relay, gbuf, terms, sbuf, rbuf, kbuf, vbuf, kt, qh, gh, qt, gt, sc, dp, dk, dv, starts, top, inverse, mixed,
-    back_s, back_r, dir_s, dir_r, loads, local, as_, ar_, gs_, gr_, ss_, sr_, ks_, kr_, bs_, br_, ds_, dr_,
+    back_s, back_r, loads, local, as_, ar_, gs_, gr_, ss_, sr_, ks_, kr_, bs_, br_,
 ):
     place = Place()
     acts = Acts(place, act, abuf, relay, local, as_, ar_)
@@ -440,7 +418,6 @@
     scatter = Scatter(place, terms, sbuf, rbuf, ss_, sr_)
     span = Span(place, kbuf, vbuf, ks_, kr_)
     back = Return(place, (dk, dv), back_s, back_r, bs_, br_)
-    direct = Direct(place, 2, terms, dir_s, dir_r, ds_, dr_)
     heads, tokens = qh.shape[0], qh.shape[1]
     first = place.c * tokens
     base = first - SPAN * tokens
@@ -496,23 +473,18 @@
 
     def last(h):
         score_grads(h, vbuf, kt, qh, gt, sc, dp, inverse, mixed, dk, gbuf)
-        gather.start(h)
-
-        @pl.when(h == 1)
+
+        @pl.when(h < 2)
         def _():
-            back.start(1, 1)
-
-        @pl.when(h == 2)
-        def _():
-            acts.spread()
+            gather.start(h)
 
     each_head(turn)
     span.copy(0, 0).wait_recv()
     span.copy(0, 1).start()
+    acts.start()
     each_head(own)
     span.copy(1, 0).wait_recv()
     span.copy(1, 1).start()
-    acts.start()
     each_head(middle)
     for n in (2, 3, 4, 5):
         kt[n] = kbuf[n].T
@@ -522,57 +494,63 @@
     each_head(far)
     back.start(1, 0)
     acts.forward()
+    acts.spread(1)
+    acts.spread(3)
     span.copy(1, 1).wait_recv()
     each_head(last)
     back.start(0, 0)
+    back.start(1, 1)
+    gather.start(2)
+    gather.start(3)
+    acts.spread(2)
     gather.forward(0)
     back.landed(1, 1.0, gbuf, 5 * HEAD_SIZE)
     gather.start(5)
+    acts.spread_on(1)
+    acts.spread_on(3)
     gather.forward(1)
     back.start(0, 1)
     gather.forward(2)
-    acts.spread_on()
+    acts.spread_on(2)
+    acts.spread_last(1)
+    acts.spread_last(3)
     gather.forward(3)
     back.landed(0, HEAD_SIZE**-0.5, gbuf, 4 * HEAD_SIZE)
     gather.start(4)
-    acts.spread_last()
+    acts.spread_last(2)
     gather.forward(5)
     gather.landed(0)
     gather.landed(1)
     acts.landed()
     weight_terms(0, abuf, gbuf, terms)
     scatter.step(0, 0)
+    gather.forward(4)
     gather.landed(2)
     gather.landed(3)
     weight_terms(1, abuf, gbuf, terms)
     scatter.step(1, 0)
-    gather.forward(4)
     scatter.step(0, 1)
     gather.landed(5)
-    weight_terms(3, abuf, gbuf, terms)
-    scatter.step(3, 0)
+    gather.landed(4)
+    weight_terms(2, abuf, gbuf, terms)
+    scatter.step(2, 0)
     scatter.step(1, 1)
     scatter.step(0, 2)
-    gather.landed(4)
-    weight_terms(2, abuf, gbuf, terms)
-    direct.start()
-    scatter.step(3, 1)
+    scatter.step(2, 1)
     scatter.step(1, 2)
     scatter.step(0, 3)
-    scatter.step(3, 2)
+    scatter.step(2, 2)
     scatter.step(1, 3)
     out[0:WIDE, :] = scatter.result(0)
-    scatter.step(3, 3)
+    scatter.step(2, 3)
     out[WIDE : 2 * WIDE, :] = scatter.result(1)
-    out[4 * HEAD_SIZE : 5 * HEAD_SIZE, :] = direct.result()
-    out[5 * HEAD_SIZE : 6 * HEAD_SIZE, :] = scatter.result(3)
+    out[2 * WIDE : 3 * WIDE, :] = scatter.result(2)
     acts.finish()
     span.finish()
     back.finish()
-    direct.finish()
     for n in range(heads + 2):
         gather.finish(n)
-    for group in (0, 1, 3):
+    for group in range(len(PARTS)):
         scatter.finish(group)
 
 
@@ -624,12 +602,10 @@
             pltpu.VMEM((heads, 1, tokens), f32),
             pltpu.VMEM((2, 2, 2, WIDE, HEAD_SIZE), bf16),
             pltpu.VMEM((2, 2, 2, WIDE, HEAD_SIZE), bf16),
-            pltpu.VMEM((NZ - 1, HEAD_SIZE, chunk), bf16),
-            pltpu.VMEM((NZ - 1, HEAD_SIZE, chunk), bf16),
             dma((2 + 2 * heads,)),
             dma,
-            dma((15,)),
-            dma((15,)),
+            dma((8 * NX,)),
+            dma((8 * NX,)),
             dma((heads + 2, 4)),
             dma((heads + 2, 4)),
             dma((len(PARTS), 2, NZ // 2)),
@@ -638,8 +614,6 @@
             dma((2, 2)),
             dma((2, 2)),
             dma((2, 2)),
-            dma((NZ - 1,)),
-            dma((NZ - 1,)),
         ],
         compiler_params=pltpu.CompilerParams(
             collective_id=0, has_side_effects=True, vmem_limit_bytes=56 * 2**20

time: 84.9 us -> 82.2 us (0.968)
  Pallas kernels: 83 us -> 81 us
    pallas_call x1, Pallas kernels: 81.3 us -> 79.3 us  [shards(): pl.pallas_call(kernel, out_shape=jax.ShapeDtypeStruct((width, chunk), bf1...]
where the time goes in v5:
time: 82.2 us; the launch traced here: 81.7 us
  Pallas kernels  81 us (99%)
    pallas_call x1, Pallas kernels, shards(): pl.pallas_call(kernel, out_shape=jax.ShapeDtypeStruct((width, chunk), bf1...  79.3 us
    pallas_call x1, Pallas kernels, shards(): pl.pallas_call(turned, out_shape=(jax.ShapeDtypeStruct((chunk, heads * HE...  1.7 us

profile of v5, /device:TPU:32, one launch (start us, length us, event | category | flops | bytes accessed | tf_op | source)
XLA Modules:
  0.0 81.7 jit_solution(2603785283101918322)
XLA Ops:
  0.6 79.3 %shard_map.85.total = bf16[768,128]{1,0:T(8,128)(2,1)} custom-call(s32[32]{0:T(128)} %docs.1, bf16[512,4096]{1,0:T(8,128)(2,1)} %act.1, bf16[512,512]{1,0:T(8,128)(2,1)} %q.1, bf16[2,256,128]{2,1,0:T(8,128)(2,1)} %bitcast.2, bf16[2,256,128]{2,1,0:T(8,128)(2,1)} %bitcast.3, bf16[512,512]{1,0:T(8,128)(2,1)} %g.1), custom_call_target="tpu_custom_call" | custom-call | tf_op jit(solution)/shard_map/pallas_call | solution.py:576
  80.0 1.7 %shard_map.86 = (bf16[128,512]{1,0:T(8,128)(2,1)}, bf16[128,128]{1,0:T(8,128)(2,1)}, bf16[128,128]{1,0:T(8,128)(2,1)}) custom-call(bf16[768,128]{1,0:T(8,128)(2,1)} %shard_map.85.total), custom_call_target="tpu_custom_call" | custom-call | tf_op jit(solution)/shard_map/pallas_call | solution.py:629

commit v6 on v5

--- a/solution.py
+++ b/solution.py
@@ -522,9 +522,9 @@
     gather.landed(0)
     gather.landed(1)
     acts.landed()
+    gather.forward(4)
     weight_terms(0, abuf, gbuf, terms)
     scatter.step(0, 0)
-    gather.forward(4)
     gather.landed(2)
     gather.landed(3)
     weight_terms(1, abuf, gbuf, terms)

time: 82.2 us -> 83.4 us (1.015)
  Pallas kernels: 81 us -> 82 us
    pallas_call x1, Pallas kernels: 79.3 us -> 80.3 us  [shards(): pl.pallas_call(kernel, out_shape=jax.ShapeDtypeStruct((width, chunk), bf1...]
where the time goes in v6:
time: 83.4 us; the launch traced here: 82.7 us
  Pallas kernels  82 us (98%)
    pallas_call x1, Pallas kernels, shards(): pl.pallas_call(kernel, out_shape=jax.ShapeDtypeStruct((width, chunk), bf1...  80.3 us
    pallas_call x1, Pallas kernels, shards(): pl.pallas_call(turned, out_shape=(jax.ShapeDtypeStruct((chunk, heads * HE...  1.7 us

profile of v6, /device:TPU:32, one launch (start us, length us, event | category | flops | bytes accessed | tf_op | source)
XLA Modules:
  0.0 82.7 jit_solution(17517285532801988533)
XLA Ops:
  0.6 80.3 %shard_map.85.total = bf16[768,128]{1,0:T(8,128)(2,1)} custom-call(s32[32]{0:T(128)} %docs.1, bf16[512,4096]{1,0:T(8,128)(2,1)} %act.1, bf16[512,512]{1,0:T(8,128)(2,1)} %q.1, bf16[2,256,128]{2,1,0:T(8,128)(2,1)} %bitcast.2, bf16[2,256,128]{2,1,0:T(8,128)(2,1)} %bitcast.3, bf16[512,512]{1,0:T(8,128)(2,1)} %g.1), custom_call_target="tpu_custom_call" | custom-call | tf_op jit(solution)/shard_map/pallas_call | solution.py:576
  81.0 1.7 %shard_map.86 = (bf16[128,512]{1,0:T(8,128)(2,1)}, bf16[128,128]{1,0:T(8,128)(2,1)}, bf16[128,128]{1,0:T(8,128)(2,1)}) custom-call(bf16[768,128]{1,0:T(8,128)(2,1)} %shard_map.85.total), custom_call_target="tpu_custom_call" | custom-call | tf_op jit(solution)/shard_map/pallas_call | solution.py:629
